TPU v7x, 256 devices: a whole 4x4x8 slice. The times are simulated.
256 devices in a mesh: rows: 32 (over z, x), pairs: 8 (over y, core).
Axes of the slice: x: 4, y: 4, z: 8, core: 2. Of those that a mesh axis runs over, the one named last changes fastest.
Arguments:
- snapshot: float32 [32768, 8192], P('rows', 'pairs')
- plan: int32 [2, 8, 8], P(None, 'pairs'), may hold values from 0 to 7, each once within a row
Outputs:
- rotated: float32 [32768, 8192], P('rows', 'pairs')
Inputs may be any that keep to these rules, and one draw needn't show every extreme that they name: Each plan[s, q, :] holds every local place exactly once.
All inputs are finite; a program needn't handle non-finite values.
Results may differ from a plain program's by a relative error of at most 0.0003.
Values sent between devices are 32-bit elements; how exact they have to be, the bound alone decides.
No kernel may reach another device: no remote copies, remote signals or barrier semaphores. Data moves between devices by JAX's collectives and lax.ppermute only.
A program may use at most 128 MiB of HBM per device.

v0:
```python
import jax
import jax.numpy as jnp
from jax import lax
from jax.sharding import PartitionSpec as P


def passed_along(value, axis, steps):
    count = lax.axis_size(axis)
    pairs = [(source, (source + steps) % count) for source in range(count)]
    return lax.ppermute(value, axis, pairs)


def cayley_rotation(cross, norms, width):
    scale = lax.rsqrt(norms + 1e-06)
    half = 0.5 * cross * scale[:, :width, None] * scale[:, None, width:]
    count = cross.shape[0]
    zeros = jnp.zeros((count, width, width), jnp.float32)
    upper = jnp.concatenate([zeros, half], axis=2)
    lower = jnp.concatenate([-jnp.swapaxes(half, 1, 2), zeros], axis=2)
    skew = jnp.concatenate([upper, lower], axis=1)
    eye_big = jnp.eye(2 * width, dtype=jnp.float32)
    eye_small = jnp.eye(width, dtype=jnp.float32)
    hp = lax.Precision.HIGHEST
    square = eye_big + 2.0 * skew + jnp.einsum("pij,pjk->pik", skew, skew, precision=hp)
    first = eye_small + jnp.einsum("pij,pkj->pik", half, half, precision=hp)
    second = eye_small + jnp.einsum("pji,pjk->pik", half, half, precision=hp)

    def solve_block(spd, rhs):
        factor = jnp.linalg.cholesky(spd)
        return jax.scipy.linalg.cho_solve((factor, True), rhs)

    left_cols = jax.vmap(solve_block)(first, jnp.swapaxes(square[:, :, :width], 1, 2))
    right_cols = jax.vmap(solve_block)(second, jnp.swapaxes(square[:, :, width:], 1, 2))
    return jnp.concatenate([jnp.swapaxes(left_cols, 1, 2), jnp.swapaxes(right_cols, 1, 2)], axis=2)


def local(snapshot, plan):
    hp = lax.Precision.HIGHEST
    height, total = snapshot.shape
    nblocks = plan.shape[2]
    width = total // nblocks
    npair = nblocks // 2
    blocks = snapshot.reshape(height, nblocks, width)
    for step in range(plan.shape[0]):
        blocks = jnp.take(blocks, plan[step, 0], axis=1)
        paired = blocks.reshape(height, npair, 2 * width)
        gram = jnp.einsum("rpi,rpj->pij", paired, paired, precision=hp)
        gram = lax.psum(gram, "rows")
        cross = gram[:, :width, width:]
        norms = jnp.diagonal(gram, axis1=1, axis2=2)
        rotation = cayley_rotation(cross, norms, width)
        turned = jnp.einsum("rpi,pij->rpj", paired, rotation, precision=hp)
        turned = turned.reshape(height, npair, 2, width)
        moved = passed_along(turned[:, :, 1], "pairs", 1)
        blocks = jnp.stack([turned[:, :, 0], moved], axis=2).reshape(height, nblocks, width)
    return blocks.reshape(height, total)


def solution(mesh):
    return jax.shard_map(
        local,
        mesh=mesh,
        in_specs=(P("rows", "pairs"), P(None, "pairs", None)),
        out_specs=P("rows", "pairs"),
        check_vma=False,
    )
```

profile of v0, /device:TPU:2, one launch (start us, length us, event | category | flops | bytes accessed | tf_op | source)
XLA Modules:
  0.0 858.0 jit_solution(152439658183786393)
XLA Ops:
  7.2 5.3 copy.146
  12.6 5.3 copy.147
  27.4 5.4 copy.148
  32.8 8.4 fusion.43
  41.9 150.6 %all-reduce.7.cloned.1.call-done = f32[4,256,256]{2,1,0:T(8,128)} async-done(((f32[4,256,256]{2,1,0:T(8,128)}), f32[4,256,256]{2,1,0:T(8,128)}) %all-reduce.7.cloned.1.call-update) | async-done | bytes 1048592 | tf_op jit(solution)/shard_map/psum | solution.py:48
  192.5 17.4 %copy.150 = f32[4,256,256]{0,2,1:T(8,128)} copy(f32[4,256,256]{2,1,0:T(8,128)} %all-reduce.7.cloned.1.call-done) | data formatting | bytes 2097152 | tf_op jit(solution)/shard_map/psum | solution.py:48
  215.0 46.9 %custom-call.20 = f32[4,128,128]{2,1,0:T(8,128)S(1)} custom-call(f32[4,128,128]{2,1,0:T(8,128)S(1)} %fusion.26), custom_call_target="Cholesky" | custom-call | tf_op jit(solution)/shard_map/vmap(jit(cholesky))/cholesky | solution.py:29
  262.1 46.9 %custom-call.18 = f32[4,128,128]{2,1,0:T(8,128)S(1)} custom-call(f32[4,128,128]{2,1,0:T(8,128)S(1)} %fusion.29), custom_call_target="Cholesky" | custom-call | tf_op jit(solution)/shard_map/vmap(jit(cholesky))/cholesky | solution.py:29
  309.4 39.5 %custom-call.19 = f32[4,1,128,128]{2,3,1,0:T(8,128)S(1)} custom-call(f32[4,1,128,128]{3,2,1,0:T(8,128)S(1)} %get-tuple-element.26), custom_call_target="InvertDiagBlocksLowerTriangular" | custom-call | tf_op jit(solution)/shard_map/vmap(jit(_cho_solve))/triangular_solve | solution.py:30
  351.2 39.3 %custom-call.21 = f32[4,1,128,128]{2,3,1,0:T(8,128)S(1)} custom-call(f32[4,1,128,128]{3,2,1,0:T(8,128)S(1)} %get-tuple-element.27), custom_call_target="InvertDiagBlocksLowerTriangular" | custom-call | tf_op jit(solution)/shard_map/vmap(jit(_cho_solve))/triangular_solve | solution.py:30
  391.8 5.4 fusion
  403.7 25.1 %collective-permute-done = f32[1024,4,128]{2,0,1:T(8,128)} collective-permute-done((f32[1024,4,128]{2,0,1:T(8,128)}, f32[1024,4,128]{2,0,1:T(8,128)}, u32[]{:S(2)}, u32[]{:S(2)}) %collective-permute-start) | collective-permute-done | bytes 2097184 | tf_op jit(solution)/shard_map/ppermute | solution.py:10
  442.8 5.6 copy.166
  448.4 8.4 fusion.44
  456.9 145.8 %all-reduce.9.cloned.1.call-done = f32[4,256,256]{2,1,0:T(8,128)} async-done(((f32[4,256,256]{2,1,0:T(8,128)}), f32[4,256,256]{2,1,0:T(8,128)}) %all-reduce.9.cloned.1.call-update) | async-done | bytes 1048592 | tf_op jit(solution)/shard_map/psum | solution.py:48
  602.6 17.4 %copy.168 = f32[4,256,256]{0,2,1:T(8,128)} copy(f32[4,256,256]{2,1,0:T(8,128)} %all-reduce.9.cloned.1.call-done) | data formatting | bytes 2097152 | tf_op jit(solution)/shard_map/psum | solution.py:48
  625.1 46.9 %custom-call.24 = f32[4,128,128]{2,1,0:T(8,128)S(1)} custom-call(f32[4,128,128]{2,1,0:T(8,128)S(1)} %fusion.20), custom_call_target="Cholesky" | custom-call | tf_op jit(solution)/shard_map/vmap(jit(cholesky))/cholesky | solution.py:29
  672.2 47.3 %custom-call.22 = f32[4,128,128]{2,1,0:T(8,128)S(1)} custom-call(f32[4,128,128]{2,1,0:T(8,128)S(1)} %fusion.23), custom_call_target="Cholesky" | custom-call | tf_op jit(solution)/shard_map/vmap(jit(cholesky))/cholesky | solution.py:29
  720.0 39.3 %custom-call.23 = f32[4,1,128,128]{2,3,1,0:T(8,128)S(1)} custom-call(f32[4,1,128,128]{3,2,1,0:T(8,128)S(1)} %get-tuple-element.24), custom_call_target="InvertDiagBlocksLowerTriangular" | custom-call | tf_op jit(solution)/shard_map/vmap(jit(_cho_solve))/triangular_solve | solution.py:30
  761.6 39.3 %custom-call.25 = f32[4,1,128,128]{2,3,1,0:T(8,128)S(1)} custom-call(f32[4,1,128,128]{3,2,1,0:T(8,128)S(1)} %get-tuple-element.25), custom_call_target="InvertDiagBlocksLowerTriangular" | custom-call | tf_op jit(solution)/shard_map/vmap(jit(_cho_solve))/triangular_solve | solution.py:30
  802.1 5.6 fusion.4
  808.3 26.7 %collective-permute-done.1 = f32[1024,4,128]{0,2,1:T(8,128)S(1)} collective-permute-done((f32[1024,4,128]{0,2,1:T(8,128)S(1)}, f32[1024,4,128]{0,2,1:T(8,128)S(1)}, u32[]{:S(2)}, u32[]{:S(2)}) %collective-permute-start.1) | collective-permute-done | bytes 2097184 | tf_op jit(solution)/shard_map/ppermute | solution.py:10
  837.3 7.3 copy.183
  844.5 6.4 reshape_reshape.3
  (65 shorter events, 52.6 us)
Async XLA Ops:
  6.5 186.0 %all-reduce.7.cloned.1.call-start = ((), (), s32[]{:S(2)}) async-start(), calls=%async_computation | async-start | bytes 2097152 | tf_op jit(solution)/shard_map/psum | solution.py:48
  41.3 561.4 %all-reduce.9.cloned.1.call-start = ((), (), s32[]{:S(2)}) async-start(), calls=%async_computation.1 | async-start | bytes 2097152 | tf_op jit(solution)/shard_map/psum | solution.py:48
  401.8 27.0 %collective-permute-start = (f32[1024,4,128]{2,0,1:T(8,128)}, f32[1024,4,128]{2,0,1:T(8,128)}, u32[]{:S(2)}, u32[]{:S(2)}) collective-permute-start(f32[1024,4,128]{2,0,1:T(8,128)} %bitcast.126), channel_id=1, source_target_pairs={{0,1},{1,2},{2,3},{3,4},{4,5},{5,6},{6,7},{7,0},{8,9},{9,10},{10,1... | collective-permute-start | bytes 6291464 | tf_op jit(solution)/shard_map/ppermute | solution.py:10
  808.3 26.7 %collective-permute-start.1 = (f32[1024,4,128]{0,2,1:T(8,128)S(1)}, f32[1024,4,128]{0,2,1:T(8,128)S(1)}, u32[]{:S(2)}, u32[]{:S(2)}) collective-permute-start(f32[1024,4,128]{0,2,1:T(8,128)S(1)} %get-tuple-element.21), channel_id=1, source_target_pairs={{0,1},{1,2},{2,3},{3,4},{4,5},{5,6},{6,7},{7,0},{8,9},{9,10},{10,1... | collective-permute-start | bytes 6291464 | tf_op jit(solution)/shard_map/ppermute | solution.py:10
Sparse Core Ops, SparseCore 0:
  41.4 151.0 all-reduce.6
  457.0 145.6 all-reduce.8
where the time goes:
time: 864 us; the launch traced here: 858 us
  other arithmetic  365 us (42%)
  waiting for transfers between devices  348 us (40%)
  local copies, waits for them, and re-layouts  92.7 us (11%)
  matrix products  37.2 us (4%)
  between operations  13.9 us (2%)
    psum x2, waiting for transfers between devices, local(): gram = lax.psum(gram, 'rows')  296 us
    another operation x11, other arithmetic, solve_block(): factor = jnp.linalg.cholesky(spd)  189 us
    another operation x7, other arithmetic, solve_block(): return jax.scipy.linalg.cho_solve((factor, True), rhs)  158 us
    ppermute x2, waiting for transfers between devices, passed_along(): return lax.ppermute(value, axis, pairs)  51.8 us
    psum x2, local copies, waits for them, and re-layouts, local(): gram = lax.psum(gram, 'rows')  34.8 us
  transfers between devices with their start and end apart: 4, of which 4 were waited for; matrix products, arithmetic and copies ran while one was open for 0% of the time, Pallas kernels for 0%

commit v1 on v0

v1 whole, which is shorter than its diff:
```python
import functools

import jax
import jax.numpy as jnp
from jax import lax
from jax.experimental import pallas as pl
from jax.experimental.pallas import tpu as pltpu
from jax.sharding import PartitionSpec as P

WIDTH = 128
PAIRS = 4
PANEL = 32
GROUP_ROWS = 136
HP = lax.Precision.HIGHEST
PARAMS = pltpu.CompilerParams(vmem_limit_bytes=48 * 1024 * 1024)


def split(value):
    high = value.astype(jnp.bfloat16)
    low = (value - high.astype(jnp.float32)).astype(jnp.bfloat16)
    return high, low


def dot3(left, right, dims):
    def one(a, b):
        return lax.dot_general(a, b, (dims, ((), ())), preferred_element_type=jnp.float32)

    return one(left[0], right[0]) + (one(left[0], right[1]) + one(left[1], right[0]))


def pick(plan_ref, place, sources, target, sem):
    block = plan_ref[place]
    if len(sources) == 1:
        start = pl.multiple_of(block * WIDTH, WIDTH)
        pltpu.make_async_copy(sources[0].at[:, pl.ds(start, WIDTH)], target, sem).start()
        return
    start = pl.multiple_of((block // 2) * WIDTH, WIDTH)
    for odd, source in enumerate(sources):

        @pl.when(block % 2 == odd)
        def _():
            pltpu.make_async_copy(source.at[:, pl.ds(start, WIDTH)], target, sem).start()


def picked(sources, target, sem):
    pltpu.make_async_copy(sources[0].at[:, pl.ds(0, WIDTH)], target, sem).wait()


def gram_kernel(nsrc, plan_ref, *refs):
    sources, (out_ref, held, sems) = refs[:nsrc], refs[nsrc:]
    for place in range(2 * PAIRS):
        pick(plan_ref, place, sources, held.at[place], sems.at[place])
    line = lax.broadcasted_iota(jnp.int32, (8, WIDTH), 0)
    for pair in range(PAIRS):
        for place in (2 * pair, 2 * pair + 1):
            picked(sources, held.at[place], sems.at[place])
        first, second = held[2 * pair], held[2 * pair + 1]
        out_ref[pair, :WIDTH, :] = lax.dot_general(
            first, second, (((0,), (0,)), ((), ())), precision=HP, preferred_element_type=jnp.float32
        )
        norm_first = jnp.sum(first * first, axis=0, keepdims=True)
        norm_second = jnp.sum(second * second, axis=0, keepdims=True)
        out_ref[pair, WIDTH:, :] = jnp.where(line == 0, norm_first, jnp.where(line == 1, norm_second, 0.0))


def gram(order, sources):
    height = sources[0].shape[0]
    return pl.pallas_call(
        functools.partial(gram_kernel, len(sources)),
        out_shape=jax.ShapeDtypeStruct((PAIRS, GROUP_ROWS, WIDTH), jnp.float32),
        in_specs=[pl.BlockSpec(memory_space=pltpu.SMEM)] + [pl.BlockSpec(memory_space=pl.ANY)] * len(sources),
        out_specs=pl.BlockSpec(memory_space=pltpu.VMEM),
        scratch_shapes=[
            pltpu.VMEM((2 * PAIRS, height, WIDTH), jnp.float32),
            pltpu.SemaphoreType.DMA((2 * PAIRS,)),
        ],
        compiler_params=PARAMS,
        name="gram",
    )(order, *sources)


def panel_inverse(block):
    row = lax.broadcasted_iota(jnp.int32, block.shape, 0)
    lane = lax.broadcasted_iota(jnp.int32, block.shape, 1)
    base = (lane // PANEL) * PANEL
    inner = lane - base
    for j in range(PANEL):
        column = jnp.take_along_axis(block, base + j, axis=1)
        inverse = 1.0 / column[j : j + 1, :]
        at_j = inner == j
        line = jnp.where(at_j[j : j + 1, :], inverse, block[j : j + 1, :] * inverse)
        block = jnp.where(row == j, line, jnp.where(at_j, 0.0, block) - column * line)
    return block


def rotations(sums, count):
    width = WIDTH
    row = lax.broadcasted_iota(jnp.int32, (width, width), 0)
    lane = lax.broadcasted_iota(jnp.int32, (width, width), 1)
    eye = (row == lane).astype(jnp.float32)
    halves, systems = [], []
    for pair in range(count):
        cross = sums[pair, :width, :]
        scale = lax.rsqrt(sums[pair, width:, :] + 1e-06)
        down = jnp.sum(eye * scale[0:1, :], axis=1, keepdims=True)
        half = 0.5 * cross * down * scale[1:2, :]
        spd = eye + lax.dot_general(half, half, (((1,), (1,)), ((), ())), precision=HP, preferred_element_type=jnp.float32)
        halves.append(half)
        systems.append((spd, half))
    group = lane // PANEL
    for panel in range(width // PANEL):
        lo, hi = panel * PANEL, (panel + 1) * PANEL
        packed = None
        for pair in range(count):
            part = systems[pair][0][lo:hi, :]
            shift = (pair * PANEL - lo) % width
            if shift:
                part = pltpu.roll(part, shift, 1)
            packed = part if packed is None else jnp.where(group[:PANEL] == pair, part, packed)
        inverse = panel_inverse(packed)
        spread = jnp.where(row // PANEL == group, jnp.concatenate([inverse] * PAIRS, axis=0), 0.0)
        in_panel = group[:PANEL] == panel
        tops = [jnp.where(in_panel, eye[lo:hi, :], systems[pair][0][lo:hi, :]) for pair in range(count)]
        fill = [jnp.zeros((PANEL, width), jnp.float32)] * (PAIRS - count)
        stacked = [
            jnp.concatenate(tops + fill, axis=0),
            jnp.concatenate([systems[pair][1][lo:hi, :] for pair in range(count)] + fill, axis=0),
        ]
        fresh = [jnp.dot(spread, side, precision=HP, preferred_element_type=jnp.float32) for side in stacked]
        row_in = row // PANEL == panel
        nothing_above = [jnp.zeros((lo, width), jnp.float32)] if lo else []
        nothing_below = [jnp.zeros((width - hi, width), jnp.float32)] if hi < width else []
        done = []
        for pair in range(count):
            spd, rest = systems[pair]
            sides = []
            for side, new in zip((jnp.where(group == panel, 0.0, spd), rest), fresh):
                mine = new[pair * PANEL : (pair + 1) * PANEL, :]
                placed = jnp.concatenate(nothing_above + [mine] + nothing_below, axis=0)
                change = jnp.dot(spd, placed, precision=HP, preferred_element_type=jnp.float32)
                sides.append(jnp.where(row_in, placed, side - change))
            done.append(tuple(sides))
        systems = done
    return [(halves[pair],) + systems[pair] for pair in range(count)]


def turn_kernel(nsrc, plan_ref, sums_ref, *refs):
    sources, (stay_ref, moved_ref, held, stay, moved, in_sems, out_sems) = refs[:nsrc], refs[nsrc:]
    for place in range(2 * PAIRS):
        pick(plan_ref, place, sources, held.at[place], in_sems.at[place])
    width = WIDTH
    row = lax.broadcasted_iota(jnp.int32, (width, width), 0)
    lane = lax.broadcasted_iota(jnp.int32, (width, width), 1)
    eye = (row == lane).astype(jnp.float32)
    solved = rotations(sums_ref, PAIRS)
    every = ((1,), (0,))
    copies = []
    stride = stay_ref.shape[1] // PAIRS
    for pair in range(PAIRS):
        half, inverse, across = solved[pair]
        top_left = 2.0 * inverse - eye
        top_right = 2.0 * across
        bottom_right = eye - 2.0 * lax.dot_general(
            half, across, (((0,), (0,)), ((), ())), precision=HP, preferred_element_type=jnp.float32
        )
        rotation = jnp.concatenate(
            [
                jnp.concatenate([top_left, top_right], axis=1),
                jnp.concatenate([-top_right.T, bottom_right], axis=1),
            ],
            axis=0,
        )
        for place in (2 * pair, 2 * pair + 1):
            picked(sources, held.at[place], in_sems.at[place])
        both = jnp.concatenate([held[2 * pair], held[2 * pair + 1]], axis=1)
        turned = dot3(split(both), split(rotation), every)
        stay[pair] = turned[:, :width]
        moved[pair] = turned[:, width:]
        copies.append(
            pltpu.make_async_copy(moved.at[pair], moved_ref.at[:, pl.ds(pair * width, width)], out_sems.at[2 * pair])
        )
        copies[-1].start()
        copies.append(
            pltpu.make_async_copy(stay.at[pair], stay_ref.at[:, pl.ds(pair * stride, width)], out_sems.at[2 * pair + 1])
        )
        copies[-1].start()
    for copy in copies:
        copy.wait()


def turn(order, sums, sources, last):
    height = sources[0].shape[0]
    across = PAIRS * WIDTH
    blocks = (PAIRS, height, WIDTH)
    return pl.pallas_call(
        functools.partial(turn_kernel, len(sources)),
        out_shape=(
            jax.ShapeDtypeStruct((height, 2 * across if last else across), jnp.float32),
            jax.ShapeDtypeStruct((height, across), jnp.float32),
        ),
        in_specs=[pl.BlockSpec(memory_space=pltpu.SMEM), pl.BlockSpec(memory_space=pltpu.VMEM)]
        + [pl.BlockSpec(memory_space=pl.ANY)] * len(sources),
        out_specs=[pl.BlockSpec(memory_space=pl.ANY)] * 2,
        scratch_shapes=[
            pltpu.VMEM((2 * PAIRS, height, WIDTH), jnp.float32),
            pltpu.VMEM(blocks, jnp.float32),
            pltpu.VMEM(blocks, jnp.float32),
            pltpu.SemaphoreType.DMA((2 * PAIRS,)),
            pltpu.SemaphoreType.DMA((2 * PAIRS,)),
        ],
        compiler_params=PARAMS,
        name="turn",
    )(order, sums, *sources)


def fill_kernel(moved_ref, _, out_ref, sems):
    copies = [
        pltpu.make_async_copy(
            moved_ref.at[:, pl.ds(pair * WIDTH, WIDTH)],
            out_ref.at[:, pl.ds((2 * pair + 1) * WIDTH, WIDTH)],
            sems.at[pair],
        )
        for pair in range(PAIRS)
    ]
    for copy in copies:
        copy.start()
    for copy in copies:
        copy.wait()


def fill(moved, out):
    return pl.pallas_call(
        fill_kernel,
        out_shape=jax.ShapeDtypeStruct(out.shape, out.dtype),
        in_specs=[pl.BlockSpec(memory_space=pl.ANY)] * 2,
        out_specs=pl.BlockSpec(memory_space=pl.ANY),
        scratch_shapes=[pltpu.SemaphoreType.DMA((PAIRS,))],
        input_output_aliases={1: 0},
        compiler_params=PARAMS,
        name="fill",
    )(moved, out)


def summed(parts, nx):
    count = lax.axis_size("rows")
    nz = count // nx
    beside = [[z * nx + x for x in range(nx)] for z in range(nz)]
    parts = lax.all_to_all(parts, "rows", 0, 0, axis_index_groups=beside)
    mine = jnp.sum(parts, axis=0)
    step = 1
    while step < nz:
        mine = mine + lax.ppermute(mine, "rows", [(i, (((i // nx) ^ step) * nx) + i % nx) for i in range(count)])
        step *= 2
    return lax.all_to_all(jnp.broadcast_to(mine, (nx,) + mine.shape), "rows", 0, 0, axis_index_groups=beside)


def local(snapshot, plan):
    count = lax.axis_size("pairs")
    onward = [(q, (q + 1) % count) for q in range(count)]
    sources = (snapshot,)
    steps = plan.shape[0]
    for step in range(steps):
        order = plan[step, 0]
        sums = summed(gram(order, sources), PAIRS)
        stay, moved = turn(order, sums, sources, step == steps - 1)
        sources = (stay, lax.ppermute(moved, "pairs", onward))
    return fill(sources[1], sources[0])


def solution(mesh):
    return jax.shard_map(
        local,
        mesh=mesh,
        in_specs=(P("rows", "pairs"), P(None, "pairs", None)),
        out_specs=P("rows", "pairs"),
        check_vma=False,
    )
```

time: 864 us -> 186 us (0.22)
  other arithmetic: 365 us -> 0.1 us
  waiting for transfers between devices: 348 us -> 72.6 us
  local copies, waits for them, and re-layouts: 92.7 us -> 2.9 us
  Pallas kernels: 0 us -> 51.8 us
  blocking collectives: 0 us -> 37.4 us
  matrix products: 37.2 us -> 0 us
  starting transfers between devices: 0.59 us -> 20.6 us
  between operations: 13.9 us -> 0.29 us
    another operation x20 -> x0, other arithmetic: 353 us -> none  [the longest x11 189 us: solve_block(): factor = jnp.linalg.cholesky(spd)]
    psum x2 -> x0, waiting for transfers between devices: 296 us -> none  [local(): gram = lax.psum(gram, 'rows')]
    pallas_call x0 -> x5, Pallas kernels: none -> 51.8 us  [the longest x2 42.8 us: turn(): pl.pallas_call(functools.partial(turn_kernel, len(sources)), out_shape=(j...]
    all_to_all x0 -> x4, blocking collectives: none -> 37.4 us  [the longest x2 19.2 us: summed(): parts = lax.all_to_all(parts, 'rows', 0, 0, axis_index_groups=beside)]
    psum x2 -> x0, local copies, waits for them, and re-layouts: 34.8 us -> none  [local(): gram = lax.psum(gram, 'rows')]
    dot_general x10 -> x0, matrix products: 32.4 us -> none  [the longest x2 16.8 us: local(): gram = jnp.einsum('rpi,rpj->pij', paired, paired, precision=hp)]
    ppermute x2 -> x8, waiting for transfers between devices: 51.8 us -> 72.6 us  [the longest x2 53.3 us: local(): sources = (stay, lax.ppermute(moved, 'pairs', onward))]
    ppermute x2 -> x8, starting transfers between devices: 0.02 us -> 20.6 us  [the longest x6 20.5 us: summed(): lax.ppermute(mine, 'rows', [(i, (i // nx ^ step) * nx + i % nx) for i in...]
  transfers between devices with their start and end apart: 4 -> 8, of which waited for: 4 -> 8; matrix products, arithmetic and copies ran while one was open for 0% -> 0% of each run, Pallas kernels for 0% -> 0%
where the time goes in v1:
time: 186 us
  waiting for transfers between devices  72.6 us (39%)
  Pallas kernels  51.8 us (28%)
  blocking collectives  37.4 us (20%)
  starting transfers between devices  20.6 us (11%)
  local copies, waits for them, and re-layouts  2.9 us (2%)
    ppermute x2, waiting for transfers between devices, local(): sources = (stay, lax.ppermute(moved, 'pairs', onward))  53.3 us
    pallas_call x2, Pallas kernels, turn(): pl.pallas_call(functools.partial(turn_kernel, len(sources)), out_shape=(j...  42.8 us
    ppermute x6, starting transfers between devices, summed(): lax.ppermute(mine, 'rows', [(i, (i // nx ^ step) * nx + i % nx) for i in...  20.5 us
    ppermute x6, waiting for transfers between devices, summed(): lax.ppermute(mine, 'rows', [(i, (i // nx ^ step) * nx + i % nx) for i in...  19.3 us
    all_to_all x2, blocking collectives, summed(): parts = lax.all_to_all(parts, 'rows', 0, 0, axis_index_groups=beside)  19.2 us
    all_to_all x2, blocking collectives, summed(): lax.all_to_all(jnp.broadcast_to(mine, (nx,) + mine.shape), 'rows', 0, 0,...  18.2 us
    pallas_call x2, Pallas kernels, gram(): pl.pallas_call(functools.partial(gram_kernel, len(sources)), out_shape=ja...  7.7 us
  transfers between devices with their start and end apart: 8, of which 8 were waited for; matrix products, arithmetic and copies ran while one was open for 0% of the time, Pallas kernels for 0%

profile of v1, /device:TPU:2, one launch (start us, length us, event | category | flops | bytes accessed | tf_op | source)
XLA Modules:
  0.0 185.7 jit_solution(3317333440422895745)
XLA Ops:
  0.0 0.7 slice_bitcast_fusion
  0.7 2.2 %copy-done = f32[1024,1024]{1,0:T(8,128)S(1)} copy-done((f32[1024,1024]{1,0:T(8,128)S(1)}, f32[1024,1024]{1,0:T(8,128)}, u32[]{:S(2)}) %copy-start) | copy-done | bytes 4194328
  2.9 3.8 %gram.2 = f32[4,136,128]{2,1,0:T(8,128)S(1)} custom-call(s32[8]{0:T(128)S(1)} %get-tuple-element.13.plan_ref, f32[1024,1024]{1,0:T(8,128)S(1)} %copy-done), custom_call_target="tpu_custom_call" | custom-call | tf_op jit(solution)/shard_map/gram/pallas_call | solution.py:68
  6.7 10.0 %all_to_all.20 = f32[4,136,128]{2,1,0:T(8,128)S(1)} all-to-all(f32[4,136,128]{2,1,0:T(8,128)S(1)} %gram.2), channel_id=1, replica_groups={{0,8,16,24},{32,40,48,56},{64,72,80,88},{96,104,112,120},{128,136,144,1..., dimensions={0} | all-to-all | bytes 557056 | tf_op jit(solution)/shard_map/all_to_all | solution.py:248
  16.7 2.0 %collective-permute-start = (f32[136,128]{1,0:T(8,128)S(1)}, f32[136,128]{1,0:T(8,128)S(1)}, u32[]{:S(2)}, u32[]{:S(2)}) collective-permute-start(f32[136,128]{1,0:T(8,128)S(1)} %reduce_sum.18), channel_id=1, source_target_pairs={{0,32},{8,40},{16,48},{24,56},{32,0},{40,8},{48,16},{56,24},{64,96... | collective-permute-start | bytes 208904 | tf_op jit(solution)/shard_map/ppermute | solution.py:252
  18.7 2.4 %collective-permute-done = f32[136,128]{1,0:T(8,128)S(1)} collective-permute-done((f32[136,128]{1,0:T(8,128)S(1)}, f32[136,128]{1,0:T(8,128)S(1)}, u32[]{:S(2)}, u32[]{:S(2)}) %collective-permute-start) | collective-permute-done | bytes 69664 | tf_op jit(solution)/shard_map/ppermute | solution.py:252
  21.1 3.3 %collective-permute-start.1 = (f32[136,128]{1,0:T(8,128)S(1)}, f32[136,128]{1,0:T(8,128)S(1)}, u32[]{:S(2)}, u32[]{:S(2)}) collective-permute-start(f32[136,128]{1,0:T(8,128)S(1)} %add.18), channel_id=1, source_target_pairs={{0,64},{8,72},{16,80},{24,88},{32,96},{40,104},{48,112},{56,120},{... | collective-permute-start | bytes 208904 | tf_op jit(solution)/shard_map/ppermute | solution.py:252
  24.5 2.3 %collective-permute-done.1 = f32[136,128]{1,0:T(8,128)S(1)} collective-permute-done((f32[136,128]{1,0:T(8,128)S(1)}, f32[136,128]{1,0:T(8,128)S(1)}, u32[]{:S(2)}, u32[]{:S(2)}) %collective-permute-start.1) | collective-permute-done | bytes 69664 | tf_op jit(solution)/shard_map/ppermute | solution.py:252
  26.8 8.4 %collective-permute-start.2 = (f32[136,128]{1,0:T(8,128)S(1)}, f32[136,128]{1,0:T(8,128)S(1)}, u32[]{:S(2)}, u32[]{:S(2)}) collective-permute-start(f32[136,128]{1,0:T(8,128)S(1)} %add.19), channel_id=1, source_target_pairs={{0,128},{8,136},{16,144},{24,152},{32,160},{40,168},{48,176},{56,1... | collective-permute-start | bytes 208904 | tf_op jit(solution)/shard_map/ppermute | solution.py:252
  35.2 2.3 %collective-permute-done.2 = f32[136,128]{1,0:T(8,128)S(1)} collective-permute-done((f32[136,128]{1,0:T(8,128)S(1)}, f32[136,128]{1,0:T(8,128)S(1)}, u32[]{:S(2)}, u32[]{:S(2)}) %collective-permute-start.2) | collective-permute-done | bytes 69664 | tf_op jit(solution)/shard_map/ppermute | solution.py:252
  37.5 9.1 %all_to_all.21.sums_ref = f32[4,136,128]{2,1,0:T(8,128)S(1)} all-to-all(f32[4,136,128]{2,1,0:T(8,128)S(1)} %broadcast_in_dim.6), channel_id=1, replica_groups={{0,8,16,24},{32,40,48,56},{64,72,80,88},{96,104,112,120},{128,136,144,1..., dimensions={0} | all-to-all | bytes 557056 | tf_op jit(solution)/shard_map/all_to_all | solution.py:254
  46.7 21.0 %turn.2 = (f32[1024,512]{1,0:T(8,128)S(1)}, f32[1024,512]{1,0:T(8,128)S(1)}) custom-call(s32[8]{0:T(128)S(1)} %get-tuple-element.13.plan_ref, f32[4,136,128]{2,1,0:T(8,128)S(1)} %all_to_all.21.sums_ref, f32[1024,1024]{1,0:T(8,128)} %refs_0_.3), custom_call_target="tpu_custom_call" | custom-call | tf_op jit(solution)/shard_map/turn/pallas_call | solution.py:195
  67.6 26.7 %collective-permute-done.3.refs_1_ = f32[1024,512]{1,0:T(8,128)S(1)} collective-permute-done((f32[1024,512]{1,0:T(8,128)S(1)}, f32[1024,512]{1,0:T(8,128)S(1)}, u32[]{:S(2)}, u32[]{:S(2)}) %collective-permute-start.3) | collective-permute-done | bytes 2097184 | tf_op jit(solution)/shard_map/ppermute | solution.py:266
  94.3 3.9 %gram.3 = f32[4,136,128]{2,1,0:T(8,128)S(1)} custom-call(s32[8]{0:T(128)S(1)} %get-tuple-element.14.plan_ref, f32[1024,512]{1,0:T(8,128)S(1)} %get-tuple-element.9.refs_0_, f32[1024,512]{1,0:T(8,128)S(1)} %collective-permute-done.3.refs_1_), custom_call_target="tpu_custom_call" | custom-call | tf_op jit(solution)/shard_map/gram/pallas_call | solution.py:68
  98.2 9.1 %all_to_all.22 = f32[4,136,128]{2,1,0:T(8,128)S(1)} all-to-all(f32[4,136,128]{2,1,0:T(8,128)S(1)} %gram.3), channel_id=1, replica_groups={{0,8,16,24},{32,40,48,56},{64,72,80,88},{96,104,112,120},{128,136,144,1..., dimensions={0} | all-to-all | bytes 557056 | tf_op jit(solution)/shard_map/all_to_all | solution.py:248
  107.7 5.0 %collective-permute-done.4 = f32[136,128]{1,0:T(8,128)S(1)} collective-permute-done((f32[136,128]{1,0:T(8,128)S(1)}, f32[136,128]{1,0:T(8,128)S(1)}, u32[]{:S(2)}, u32[]{:S(2)}) %collective-permute-start.4) | collective-permute-done | bytes 69664 | tf_op jit(solution)/shard_map/ppermute | solution.py:252
  112.7 0.4 collective-permute-start.5
  113.2 5.0 %collective-permute-done.5 = f32[136,128]{1,0:T(8,128)S(1)} collective-permute-done((f32[136,128]{1,0:T(8,128)S(1)}, f32[136,128]{1,0:T(8,128)S(1)}, u32[]{:S(2)}, u32[]{:S(2)}) %collective-permute-start.5) | collective-permute-done | bytes 69664 | tf_op jit(solution)/shard_map/ppermute | solution.py:252
  118.1 6.0 %collective-permute-start.6 = (f32[136,128]{1,0:T(8,128)S(1)}, f32[136,128]{1,0:T(8,128)S(1)}, u32[]{:S(2)}, u32[]{:S(2)}) collective-permute-start(f32[136,128]{1,0:T(8,128)S(1)} %add.22), channel_id=1, source_target_pairs={{0,128},{8,136},{16,144},{24,152},{32,160},{40,168},{48,176},{56,1... | collective-permute-start | bytes 208904 | tf_op jit(solution)/shard_map/ppermute | solution.py:252
  124.2 2.3 %collective-permute-done.6 = f32[136,128]{1,0:T(8,128)S(1)} collective-permute-done((f32[136,128]{1,0:T(8,128)S(1)}, f32[136,128]{1,0:T(8,128)S(1)}, u32[]{:S(2)}, u32[]{:S(2)}) %collective-permute-start.6) | collective-permute-done | bytes 69664 | tf_op jit(solution)/shard_map/ppermute | solution.py:252
  126.5 9.1 %all_to_all.23.sums_ref = f32[4,136,128]{2,1,0:T(8,128)S(1)} all-to-all(f32[4,136,128]{2,1,0:T(8,128)S(1)} %broadcast_in_dim.7), channel_id=1, replica_groups={{0,8,16,24},{32,40,48,56},{64,72,80,88},{96,104,112,120},{128,136,144,1..., dimensions={0} | all-to-all | bytes 557056 | tf_op jit(solution)/shard_map/all_to_all | solution.py:254
  135.6 21.8 %turn.3 = (f32[1024,1024]{1,0:T(8,128)}, f32[1024,512]{1,0:T(8,128)S(1)}) custom-call(s32[8]{0:T(128)S(1)} %get-tuple-element.14.plan_ref, f32[4,136,128]{2,1,0:T(8,128)S(1)} %all_to_all.23.sums_ref, f32[1024,512]{1,0:T(8,128)S(1)} %get-tuple-element.9.refs_0_, f32[1024,512]{1,0:T(8,128)} %copy-done.1), custom_call_target="tpu_custom_call" | custom-call | tf_op jit(solution)/shard_map/turn/pallas_call | solution.py:195
  157.5 26.7 %collective-permute-done.7.moved_ref = f32[1024,512]{1,0:T(8,128)S(1)} collective-permute-done((f32[1024,512]{1,0:T(8,128)S(1)}, f32[1024,512]{1,0:T(8,128)S(1)}, u32[]{:S(2)}, u32[]{:S(2)}) %collective-permute-start.7) | collective-permute-done | bytes 2097184 | tf_op jit(solution)/shard_map/ppermute | solution.py:266
  184.1 1.3 fill.1
  (16 shorter events, 0.5 us)
Async XLA Ops:
  0.7 2.2 %copy-start = (f32[1024,1024]{1,0:T(8,128)S(1)}, f32[1024,1024]{1,0:T(8,128)}, u32[]{:S(2)}) copy-start(f32[1024,1024]{1,0:T(8,128)} %refs_0_.3) | copy-start | bytes 12582916
  16.7 4.4 %collective-permute-start = (f32[136,128]{1,0:T(8,128)S(1)}, f32[136,128]{1,0:T(8,128)S(1)}, u32[]{:S(2)}, u32[]{:S(2)}) collective-permute-start(f32[136,128]{1,0:T(8,128)S(1)} %reduce_sum.18), channel_id=1, source_target_pairs={{0,32},{8,40},{16,48},{24,56},{32,0},{40,8},{48,16},{56,24},{64,96... | collective-permute-start | bytes 208904 | tf_op jit(solution)/shard_map/ppermute | solution.py:252
  21.1 5.6 %collective-permute-start.1 = (f32[136,128]{1,0:T(8,128)S(1)}, f32[136,128]{1,0:T(8,128)S(1)}, u32[]{:S(2)}, u32[]{:S(2)}) collective-permute-start(f32[136,128]{1,0:T(8,128)S(1)} %add.18), channel_id=1, source_target_pairs={{0,64},{8,72},{16,80},{24,88},{32,96},{40,104},{48,112},{56,120},{... | collective-permute-start | bytes 208904 | tf_op jit(solution)/shard_map/ppermute | solution.py:252
  26.8 10.7 %collective-permute-start.2 = (f32[136,128]{1,0:T(8,128)S(1)}, f32[136,128]{1,0:T(8,128)S(1)}, u32[]{:S(2)}, u32[]{:S(2)}) collective-permute-start(f32[136,128]{1,0:T(8,128)S(1)} %add.19), channel_id=1, source_target_pairs={{0,128},{8,136},{16,144},{24,152},{32,160},{40,168},{48,176},{56,1... | collective-permute-start | bytes 208904 | tf_op jit(solution)/shard_map/ppermute | solution.py:252
  67.6 26.7 %collective-permute-start.3 = (f32[1024,512]{1,0:T(8,128)S(1)}, f32[1024,512]{1,0:T(8,128)S(1)}, u32[]{:S(2)}, u32[]{:S(2)}) collective-permute-start(f32[1024,512]{1,0:T(8,128)S(1)} %get-tuple-element.10), channel_id=1, source_target_pairs={{0,1},{1,2},{2,3},{3,4},{4,5},{5,6},{6,7},{7,0},{8,9},{9,10},{10,1... | collective-permute-start | bytes 6291464 | tf_op jit(solution)/shard_map/ppermute | solution.py:266
  94.3 3.9 %copy-start.1 = (f32[1024,512]{1,0:T(8,128)}, f32[1024,512]{1,0:T(8,128)S(1)}, u32[]{:S(2)}) copy-start(f32[1024,512]{1,0:T(8,128)S(1)} %collective-permute-done.3.refs_1_) | copy-start | bytes 6291460
  107.4 5.4 %collective-permute-start.4 = (f32[136,128]{1,0:T(8,128)S(1)}, f32[136,128]{1,0:T(8,128)S(1)}, u32[]{:S(2)}, u32[]{:S(2)}) collective-permute-start(f32[136,128]{1,0:T(8,128)S(1)} %reduce_sum.19), channel_id=1, source_target_pairs={{0,32},{8,40},{16,48},{24,56},{32,0},{40,8},{48,16},{56,24},{64,96... | collective-permute-start | bytes 208904 | tf_op jit(solution)/shard_map/ppermute | solution.py:252
  112.7 5.4 %collective-permute-start.5 = (f32[136,128]{1,0:T(8,128)S(1)}, f32[136,128]{1,0:T(8,128)S(1)}, u32[]{:S(2)}, u32[]{:S(2)}) collective-permute-start(f32[136,128]{1,0:T(8,128)S(1)} %add.21), channel_id=1, source_target_pairs={{0,64},{8,72},{16,80},{24,88},{32,96},{40,104},{48,112},{56,120},{... | collective-permute-start | bytes 208904 | tf_op jit(solution)/shard_map/ppermute | solution.py:252
  118.1 8.3 %collective-permute-start.6 = (f32[136,128]{1,0:T(8,128)S(1)}, f32[136,128]{1,0:T(8,128)S(1)}, u32[]{:S(2)}, u32[]{:S(2)}) collective-permute-start(f32[136,128]{1,0:T(8,128)S(1)} %add.22), channel_id=1, source_target_pairs={{0,128},{8,136},{16,144},{24,152},{32,160},{40,168},{48,176},{56,1... | collective-permute-start | bytes 208904 | tf_op jit(solution)/shard_map/ppermute | solution.py:252
  157.5 26.7 %collective-permute-start.7 = (f32[1024,512]{1,0:T(8,128)S(1)}, f32[1024,512]{1,0:T(8,128)S(1)}, u32[]{:S(2)}, u32[]{:S(2)}) collective-permute-start(f32[1024,512]{1,0:T(8,128)S(1)} %get-tuple-element.11), channel_id=1, source_target_pairs={{0,1},{1,2},{2,3},{3,4},{4,5},{5,6},{6,7},{7,0},{8,9},{9,10},{10,1... | collective-permute-start | bytes 6291464 | tf_op jit(solution)/shard_map/ppermute | solution.py:266

commit v2 on v0

v2 whole, which is shorter than its diff:
```python
import functools

import jax
import jax.numpy as jnp
from jax import lax
from jax.experimental import pallas as pl
from jax.experimental.pallas import tpu as pltpu
from jax.sharding import PartitionSpec as P

WIDTH = 128
PAIRS = 4
PLACES = 2 * PAIRS
PANEL = 32
PACK = WIDTH // PANEL
SUB = 8
GROUP = 8
GROUP_ROWS = 136
HP = lax.Precision.HIGHEST
PARAMS = pltpu.CompilerParams(vmem_limit_bytes=48 * 1024 * 1024)


def split(value):
    high = value.astype(jnp.bfloat16)
    return high, (value - high.astype(jnp.float32)).astype(jnp.bfloat16)


def load_blocks(source, held, sems):
    for place in range(PLACES):
        pltpu.make_async_copy(source.at[:, pl.ds(place * WIDTH, WIDTH)], held.at[place], sems.at[place]).start()


def wait_block(source, held, sems, place):
    pltpu.make_async_copy(source.at[:, pl.ds(0, WIDTH)], held.at[place], sems.at[place]).wait()


def gram_kernel(step, x_ref, *refs):
    if step is None:
        out_ref, held, sems = refs
        load_blocks(x_ref, held, sems)
        order = list(range(PLACES))
    else:
        plan_ref, out_ref, held, sems, plan, plan_sem = refs
        load_plan = pltpu.make_async_copy(plan_ref, plan, plan_sem)
        load_plan.start()
        load_blocks(x_ref, held, sems)
        load_plan.wait()
        order = [plan[step, 0, place] for place in range(PLACES)]
    line = lax.broadcasted_iota(jnp.int32, (8, WIDTH), 0)
    for pair in range(PAIRS):
        both = order[2 * pair : 2 * pair + 2]
        for place in both:
            wait_block(x_ref, held, sems, place)
        first, second = held[both[0]], held[both[1]]
        out_ref[pair, :WIDTH, :] = lax.dot_general(
            first, second, (((0,), (0,)), ((), ())), precision=HP, preferred_element_type=jnp.float32
        )
        norm_first = jnp.sum(first * first, axis=0, keepdims=True)
        norm_second = jnp.sum(second * second, axis=0, keepdims=True)
        out_ref[pair, WIDTH:, :] = jnp.where(line == 0, norm_first, jnp.where(line == 1, norm_second, 0.0))


def gram(x, plan, step):
    planned = step is not None
    scratch = [pltpu.VMEM((PLACES, x.shape[0], WIDTH), jnp.float32), pltpu.SemaphoreType.DMA((PLACES,))]
    if planned:
        scratch += [pltpu.SMEM(plan.shape, jnp.int32), pltpu.SemaphoreType.DMA]
    return pl.pallas_call(
        functools.partial(gram_kernel, step),
        out_shape=jax.ShapeDtypeStruct((PAIRS, GROUP_ROWS, WIDTH), jnp.float32),
        in_specs=[pl.BlockSpec(memory_space=pl.ANY)] * (2 if planned else 1),
        out_specs=pl.BlockSpec(memory_space=pltpu.VMEM),
        scratch_shapes=scratch,
        compiler_params=PARAMS,
        name="gram",
    )(*((x, plan) if planned else (x,)))


def panel_inverse(block):
    parts = [block[i : i + SUB, :] for i in range(0, PANEL, SUB)]
    row = lax.broadcasted_iota(jnp.int32, (SUB, WIDTH), 0)
    lane = lax.broadcasted_iota(jnp.int32, (SUB, WIDTH), 1)
    base = (lane // PANEL) * PANEL
    inner = lane - base

    def line(value, j):
        return jnp.broadcast_to(value[j // SUB][j % SUB : j % SUB + 1, :], (SUB, WIDTH))

    def column(value, j):
        return [jnp.take_along_axis(part, base + j, axis=1) for part in value]

    for start in range(0, PANEL, GROUP):
        columns = [column(parts, j) for j in range(start, start + GROUP)]
        for j in range(start, start + GROUP, 2):
            c0, c1, *columns = columns
            a, b, d = line(c0, j), line(c1, j), line(c1, j + 1)
            r = 1.0 / (a * d - b * b)

            def update(value, u, v, cleared):
                m0, m1 = (d * u - b * v), (a * v - b * u)
                out = []
                for i in range(len(value)):
                    old = value[i] if cleared is None else jnp.where(cleared, 0.0, value[i])
                    out.append(old - (c0[i] * m0 + c1[i] * m1) * r)
                i = j // SUB
                out[i] = jnp.where(row == j % SUB, m0 * r, jnp.where(row == j % SUB + 1, m1 * r, out[i]))
                return out
            columns = [update(c, line(c, j), line(c, j + 1), None) for c in columns]
            at0, at1 = inner == j, inner == j + 1
            u = jnp.where(at0, 1.0, jnp.where(at1, 0.0, line(parts, j)))
            v = jnp.where(at1, 1.0, jnp.where(at0, 0.0, line(parts, j + 1)))
            parts = update(parts, u, v, at0 | at1)
    return jnp.concatenate(parts, axis=0)


def split3(value):
    high = value.astype(jnp.bfloat16)
    rest = value - high.astype(jnp.float32)
    middle = rest.astype(jnp.bfloat16)
    return high, middle, (rest - middle.astype(jnp.float32)).astype(jnp.bfloat16)


def contract(left, right, over):
    return lax.dot_general(left, right, (((over,), (over,)), ((), ())), preferred_element_type=jnp.float32)


def tall_dot(left, right):
    (a, b, c), (d, e, f) = left, right
    return contract(jnp.concatenate([a, b, a, b, c, a], axis=0), jnp.concatenate([d, d, e, e, d, f], axis=0), 0)


def square_dot(left, right, over):
    (a, b, c), (d, e, f) = left, right
    pair = lambda x, y: jnp.concatenate([x, y], axis=over)
    return contract(pair(a, b), pair(d, e), over) + (
        contract(pair(a, b), pair(e, d), over) + contract(pair(a, c), pair(f, d), over)
    )


def rotations(sums, count):
    width = WIDTH
    row = lax.broadcasted_iota(jnp.int32, (width, width), 0)
    lane = lax.broadcasted_iota(jnp.int32, (width, width), 1)
    eye = (row == lane).astype(jnp.float32)
    halves, systems = [], []
    for pair in range(count):
        cross = sums[pair][:width, :]
        scale = lax.rsqrt(sums[pair][width:, :] + 1e-06)
        down = jnp.sum(eye * scale[0:1, :], axis=1, keepdims=True)
        half = 0.5 * cross * down * scale[1:2, :]
        parts = split3(half)
        spd = eye + square_dot(parts, parts, 1)
        halves.append((half, parts))
        systems.append(jnp.concatenate([spd, half], axis=1))
    group = lax.broadcasted_iota(jnp.int32, (PANEL, width), 1) // PANEL
    wide = lax.broadcasted_iota(jnp.int32, (PANEL, 2 * width), 1)
    wide_row = lax.broadcasted_iota(jnp.int32, (PANEL, 2 * width), 0)
    for panel in range(width // PANEL):
        lo, hi = panel * PANEL, (panel + 1) * PANEL
        inside = (wide >= lo) & (wide < hi)
        cleared = jnp.concatenate([inside] * (width // PANEL), axis=0)
        done = []
        for first in range(0, count, PACK):
            members = range(first, min(first + PACK, count))
            packed = None
            for pair in members:
                part = systems[pair][lo:hi, :width]
                shift = ((pair - first) * PANEL - lo) % width
                if shift:
                    part = pltpu.roll(part, shift, 1)
                packed = part if packed is None else jnp.where(group == pair - first, part, packed)
            inverse = split3(panel_inverse(packed))
            for pair in members:
                old = systems[pair]
                top = old[lo:hi, :]
                unit = jnp.where(inside, (wide - lo == wide_row).astype(jnp.float32), top)
                at = (pair - first) * PANEL
                fresh = tall_dot(inverse, split3(unit))[at : at + PANEL, :]
                side = jnp.where(lane[:PANEL] < lo, -top[:, :width], top[:, :width])
                change = tall_dot(split3(side), split3(fresh))
                updated = jnp.where(cleared, 0.0, old) - change
                done.append(jnp.concatenate(([updated[:lo]] if lo else []) + [fresh] + ([updated[hi:]] if hi < width else []), axis=0))
        systems = done
    return [(halves[pair][0], systems[pair][:, :width], systems[pair][:, width:]) for pair in range(count)]


def turn_kernel(step, sums_ref, own_ref, prev_ref, *refs):
    if step is None:
        out_ref, held, sides, turned, in_sems, out_sems = refs
        plans = []
    else:
        own_plan_ref, prev_plan_ref, out_ref, held, sides, turned, in_sems, out_sems, plan, plan_sems = refs
        plans = [
            pltpu.make_async_copy(ref, plan.at[which], plan_sems.at[which])
            for which, ref in enumerate((own_plan_ref, prev_plan_ref))
        ]
        for copy in plans:
            copy.start()
    for which, ref in enumerate((own_ref, prev_ref)):
        load_blocks(ref, held.at[which], in_sems.at[which])
    width = WIDTH
    row = lax.broadcasted_iota(jnp.int32, (width, width), 0)
    lane = lax.broadcasted_iota(jnp.int32, (width, width), 1)
    eye = (row == lane).astype(jnp.float32)
    sums = [sums_ref.at[pair, which] for which in range(2) for pair in range(PAIRS)]
    for index, (half, inverse, across) in enumerate(rotations(sums, len(sums))):
        if index < PAIRS:
            top, bottom = 2.0 * inverse - eye, -2.0 * across.T
        else:
            top, bottom = 2.0 * across, eye - 2.0 * square_dot(split3(half), split3(across), 0)
        high, low = split(jnp.concatenate([top, bottom], axis=0))
        sides[index, :, :width] = high
        sides[index, :, width:] = low
    for copy in plans:
        copy.wait()
    for which, ref in enumerate((own_ref, prev_ref)):
        for place in range(PLACES):
            wait_block(ref, held.at[which], in_sems.at[which], place)
    copies = []
    for slot in range(PLACES):
        if step is None:
            which, pair = slot % 2, slot // 2
            first, second = 2 * pair, 2 * pair + 1
        else:
            place = plan[0, step + 1, 0, slot]
            which, pair = place % 2, place // 2
            first, second = plan[which, step, 0, 2 * pair], plan[which, step, 0, 2 * pair + 1]
        high, low = split(jnp.concatenate([held[which, first], held[which, second]], axis=1))
        side = sides[which * PAIRS + pair]
        parts = jnp.dot(high, side, preferred_element_type=jnp.float32)
        rest = jnp.dot(low, side[:, :width], preferred_element_type=jnp.float32)
        turned[slot] = parts[:, :width] + (parts[:, width:] + rest)
        copies.append(
            pltpu.make_async_copy(turned.at[slot], out_ref.at[:, pl.ds(slot * width, width)], out_sems.at[slot])
        )
        copies[-1].start()
    for copy in copies:
        copy.wait()


def turn(sums, own, prev, own_plan, prev_plan, step):
    planned = step is not None
    height = own.shape[0]
    scratch = [
        pltpu.VMEM((2, PLACES, height, WIDTH), jnp.float32),
        pltpu.VMEM((2 * PAIRS, 2 * WIDTH, 2 * WIDTH), jnp.bfloat16),
        pltpu.VMEM((PLACES, height, WIDTH), jnp.float32),
        pltpu.SemaphoreType.DMA((2, PLACES)),
        pltpu.SemaphoreType.DMA((PLACES,)),
    ]
    if planned:
        scratch += [pltpu.SMEM((2,) + own_plan.shape, jnp.int32), pltpu.SemaphoreType.DMA((2,))]
    return pl.pallas_call(
        functools.partial(turn_kernel, step),
        out_shape=jax.ShapeDtypeStruct(own.shape, jnp.float32),
        in_specs=[pl.BlockSpec(memory_space=pltpu.VMEM)] + [pl.BlockSpec(memory_space=pl.ANY)] * (4 if planned else 2),
        out_specs=pl.BlockSpec(memory_space=pl.ANY),
        scratch_shapes=scratch,
        compiler_params=PARAMS,
        name="turn",
    )(sums, own, prev, *((own_plan, prev_plan) if planned else ()))


def summed(parts, onward):
    nx, count = PAIRS, lax.axis_size("rows")
    nz = count // nx
    beside = [[z * nx + x for x in range(nx)] for z in range(nz)]
    parts = lax.all_to_all(parts, "rows", 0, 0, axis_index_groups=beside)
    mine = jnp.sum(parts, axis=0)
    step = 1
    while step < nz:
        mine = mine + lax.ppermute(mine, "rows", [(i, (((i // nx) ^ step) * nx) + i % nx) for i in range(count)])
        step *= 2
    both = jnp.stack([mine, lax.ppermute(mine, "pairs", onward)])
    return lax.all_to_all(jnp.broadcast_to(both, (nx,) + both.shape), "rows", 0, 0, axis_index_groups=beside)


def local(snapshot, plan):
    count = lax.axis_size("pairs")
    onward = [(q, (q + 1) % count) for q in range(count)]
    steps = plan.shape[0]
    prev_plan = lax.ppermute(plan, "pairs", onward)
    x = snapshot
    for step in range(steps):
        prev = lax.ppermute(x, "pairs", onward)
        sums = summed(gram(x, plan, step if step == 0 else None), onward)
        x = turn(sums, x, prev, plan, prev_plan, step if step == 0 else None)
    return x


def solution(mesh):
    return jax.shard_map(
        local,
        mesh=mesh,
        in_specs=(P("rows", "pairs"), P(None, "pairs", None)),
        out_specs=P("rows", "pairs"),
        check_vma=False,
    )
```

time: 864 us -> 149 us (0.17)
  other arithmetic: 365 us -> 0.13 us
  waiting for transfers between devices: 348 us -> 52.9 us
  local copies, waits for them, and re-layouts: 92.7 us -> 3.75 us
  matrix products: 37.2 us -> 0 us
  blocking collectives: 0 us -> 31.8 us
  Pallas kernels: 0 us -> 31 us
  starting transfers between devices: 0.59 us -> 28.4 us
  between operations: 13.9 us -> 0.27 us
    another operation x20 -> x2, other arithmetic: 353 us -> 0.03 us  [summed(): both = jnp.stack([mine, lax.ppermute(mine, 'pairs', onward)])]
    psum x2 -> x0, waiting for transfers between devices: 296 us -> none  [local(): gram = lax.psum(gram, 'rows')]
    psum x2 -> x0, local copies, waits for them, and re-layouts: 34.8 us -> none  [local(): gram = lax.psum(gram, 'rows')]
    dot_general x10 -> x0, matrix products: 32.4 us -> none  [the longest x2 16.8 us: local(): gram = jnp.einsum('rpi,rpj->pij', paired, paired, precision=hp)]
    all_to_all x0 -> x3, blocking collectives: none -> 31.8 us  [the longest x2 21.2 us: summed(): parts = lax.all_to_all(parts, 'rows', 0, 0, axis_index_groups=beside)]
    pallas_call x0 -> x4, Pallas kernels: none -> 31 us  [the longest x2 23.8 us: turn(): pl.pallas_call(functools.partial(turn_kernel, step), out_shape=jax.ShapeD...]
    ppermute x2 -> x11, starting transfers between devices: 0.02 us -> 22.7 us  [the longest x6 22.6 us: summed(): lax.ppermute(mine, 'rows', [(i, (i // nx ^ step) * nx + i % nx) for i in...]
    gather x4 -> x0, local copies, waits for them, and re-layouts: 14.6 us -> none  [the longest x2 9.94 us: local(): blocks = jnp.take(blocks, plan[step, 0], axis=1)]
  transfers between devices with their start and end apart: 4 -> 12, of which waited for: 4 -> 10; matrix products, arithmetic and copies ran while one was open for 0% -> 1% of each run, Pallas kernels for 0% -> 5%
where the time goes in v2:
time: 149 us; the launch traced here: 148 us
  waiting for transfers between devices  52.9 us (36%)
  blocking collectives  31.8 us (21%)
  Pallas kernels  31 us (21%)
  starting transfers between devices  28.4 us (19%)
  local copies, waits for them, and re-layouts  3.75 us (3%)
    ppermute x2, waiting for transfers between devices, summed(): both = jnp.stack([mine, lax.ppermute(mine, 'pairs', onward)])  27.6 us
    pallas_call x2, Pallas kernels, turn(): pl.pallas_call(functools.partial(turn_kernel, step), out_shape=jax.ShapeD...  23.8 us
    ppermute x6, starting transfers between devices, summed(): lax.ppermute(mine, 'rows', [(i, (i // nx ^ step) * nx + i % nx) for i in...  22.6 us
    all_to_all x2, blocking collectives, summed(): parts = lax.all_to_all(parts, 'rows', 0, 0, axis_index_groups=beside)  21.2 us
    ppermute x6, waiting for transfers between devices, summed(): lax.ppermute(mine, 'rows', [(i, (i // nx ^ step) * nx + i % nx) for i in...  18.5 us
    all_to_all x1, blocking collectives, summed(): lax.all_to_all(jnp.broadcast_to(both, (nx,) + both.shape), 'rows', 0, 0,...  10.6 us
    pallas_call x2, Pallas kernels, gram(): pl.pallas_call(functools.partial(gram_kernel, step), out_shape=jax.ShapeD...  7.2 us
    all_to_all x1, starting transfers between devices, summed(): lax.all_to_all(jnp.broadcast_to(both, (nx,) + both.shape), 'rows', 0, 0,...  5.71 us
  transfers between devices with their start and end apart: 12, of which 10 were waited for; matrix products, arithmetic and copies ran while one was open for 1% of the time, Pallas kernels for 5%

profile of v2, /device:TPU:2, one launch (start us, length us, event | category | flops | bytes accessed | tf_op | source)
XLA Modules:
  0.0 148.3 jit_solution(17618142772853956549)
XLA Ops:
  0.0 2.2 %copy-done = f32[1024,1024]{1,0:T(8,128)S(1)} copy-done((f32[1024,1024]{1,0:T(8,128)S(1)}, f32[1024,1024]{1,0:T(8,128)}, u32[]{:S(2)}) %copy-start) | copy-done | bytes 4194328
  2.9 3.3 %gram.2 = f32[4,136,128]{2,1,0:T(8,128)S(1)} custom-call(f32[1024,1024]{1,0:T(8,128)S(1)} %copy-done, s32[2,1,8]{2,1,0:T(1,128)S(1)} %copy-done.1), custom_call_target="tpu_custom_call" | custom-call | tf_op jit(solution)/shard_map/gram/pallas_call | solution.py:67
  6.2 11.0 %all_to_all.20 = f32[4,136,128]{2,1,0:T(8,128)S(1)} all-to-all(f32[4,136,128]{2,1,0:T(8,128)S(1)} %gram.2), channel_id=1, replica_groups={{0,8,16,24},{32,40,48,56},{64,72,80,88},{96,104,112,120},{128,136,144,1..., dimensions={0} | all-to-all | bytes 557056 | tf_op jit(solution)/shard_map/all_to_all | solution.py:267
  17.3 2.0 %collective-permute-start = (f32[136,128]{1,0:T(8,128)S(1)}, f32[136,128]{1,0:T(8,128)S(1)}, u32[]{:S(2)}, u32[]{:S(2)}) collective-permute-start(f32[136,128]{1,0:T(8,128)S(1)} %reduce_sum.18), channel_id=1, source_target_pairs={{0,32},{8,40},{16,48},{24,56},{32,0},{40,8},{48,16},{56,24},{64,96... | collective-permute-start | bytes 208904 | tf_op jit(solution)/shard_map/ppermute | solution.py:271
  19.3 3.0 %collective-permute-done = f32[136,128]{1,0:T(8,128)S(1)} collective-permute-done((f32[136,128]{1,0:T(8,128)S(1)}, f32[136,128]{1,0:T(8,128)S(1)}, u32[]{:S(2)}, u32[]{:S(2)}) %collective-permute-start) | collective-permute-done | bytes 69664 | tf_op jit(solution)/shard_map/ppermute | solution.py:271
  22.2 3.4 %collective-permute-start.1 = (f32[136,128]{1,0:T(8,128)S(1)}, f32[136,128]{1,0:T(8,128)S(1)}, u32[]{:S(2)}, u32[]{:S(2)}) collective-permute-start(f32[136,128]{1,0:T(8,128)S(1)} %add.18), channel_id=1, source_target_pairs={{0,64},{8,72},{16,80},{24,88},{32,96},{40,104},{48,112},{56,120},{... | collective-permute-start | bytes 208904 | tf_op jit(solution)/shard_map/ppermute | solution.py:271
  25.6 3.9 %collective-permute-done.1 = f32[136,128]{1,0:T(8,128)S(1)} collective-permute-done((f32[136,128]{1,0:T(8,128)S(1)}, f32[136,128]{1,0:T(8,128)S(1)}, u32[]{:S(2)}, u32[]{:S(2)}) %collective-permute-start.1) | collective-permute-done | bytes 69664 | tf_op jit(solution)/shard_map/ppermute | solution.py:271
  29.5 6.4 %collective-permute-start.2 = (f32[136,128]{1,0:T(8,128)S(1)}, f32[136,128]{1,0:T(8,128)S(1)}, u32[]{:S(2)}, u32[]{:S(2)}) collective-permute-start(f32[136,128]{1,0:T(8,128)S(1)} %add.19), channel_id=1, source_target_pairs={{0,128},{8,136},{16,144},{24,152},{32,160},{40,168},{48,176},{56,1... | collective-permute-start | bytes 208904 | tf_op jit(solution)/shard_map/ppermute | solution.py:271
  35.9 2.3 %collective-permute-done.2 = f32[136,128]{1,0:T(8,128)S(1)} collective-permute-done((f32[136,128]{1,0:T(8,128)S(1)}, f32[136,128]{1,0:T(8,128)S(1)}, u32[]{:S(2)}, u32[]{:S(2)}) %collective-permute-start.2) | collective-permute-done | bytes 69664 | tf_op jit(solution)/shard_map/ppermute | solution.py:271
  38.2 11.9 %collective-permute-done.3 = f32[136,128]{1,0:T(8,128)S(1)} collective-permute-done((f32[136,128]{1,0:T(8,128)S(1)}, f32[136,128]{1,0:T(8,128)S(1)}, u32[]{:S(2)}, u32[]{:S(2)}) %collective-permute-start.3) | collective-permute-done | bytes 69664 | tf_op jit(solution)/shard_map/ppermute | solution.py:273
  51.0 5.7 %all-to-all-start.1 = ((f32[4,2,136,128]{3,2,1,0:T(8,128)}), f32[4,2,136,128]{3,2,1,0:T(8,128)S(1)}, u32[]{:S(2)}, u32[]{:S(2)}) async-start(f32[4,2,136,128]{3,2,1,0:T(8,128)} %broadcast_in_dim.6), calls=%async_computation.1 | async-start | bytes 1114112 | tf_op jit(solution)/shard_map/all_to_all | solution.py:274
  56.7 4.2 %collective-permute-done.5.refs_1_ = s32[2,1,8]{2,1,0:T(1,128)S(1)} collective-permute-done((s32[2,1,8]{2,1,0:T(1,128)S(1)}, s32[2,1,8]{2,1,0:T(1,128)S(1)}, u32[]{:S(2)}, u32[]{:S(2)}) %collective-permute-start.5) | collective-permute-done | bytes 96 | tf_op jit(solution)/shard_map/ppermute | solution.py:281
  60.9 2.6 %all-to-all-done.1.sums_ref = f32[4,2,136,128]{3,2,1,0:T(8,128)S(1)} async-done(((f32[4,2,136,128]{3,2,1,0:T(8,128)}), f32[4,2,136,128]{3,2,1,0:T(8,128)S(1)}, u32[]{:S(2)}, u32[]{:S(2)}) %all-to-all-start.1) | async-done | bytes 557088 | tf_op jit(solution)/shard_map/all_to_all | solution.py:274
  63.5 11.9 %turn.2.x_ref.own_ref = f32[1024,1024]{1,0:T(8,128)} custom-call(f32[4,2,136,128]{3,2,1,0:T(8,128)S(1)} %all-to-all-done.1.sums_ref, f32[1024,1024]{1,0:T(8,128)} %own_ref.1, f32[1024,1024]{1,0:T(8,128)} %collective-permute-done.4.prev_ref, s32[2,1,8]{2,1,0:T(1,128)S(1)} %copy-done.2, s32[2,1,8]{2,1,0:T(1,128)S(1)} %collective-permute-done.5.refs_1_), custom_call_target="tpu_custom_call" | custom-call | tf_op jit(solution)/shard_map/turn/pallas_call | solution.py:252
  75.4 3.9 %gram.3 = f32[4,136,128]{2,1,0:T(8,128)S(1)} custom-call(f32[1024,1024]{1,0:T(8,128)} %turn.2.x_ref.own_ref), custom_call_target="tpu_custom_call" | custom-call | tf_op jit(solution)/shard_map/gram/pallas_call | solution.py:67
  79.3 10.2 %all_to_all.21 = f32[4,136,128]{2,1,0:T(8,128)S(1)} all-to-all(f32[4,136,128]{2,1,0:T(8,128)S(1)} %gram.3), channel_id=1, replica_groups={{0,8,16,24},{32,40,48,56},{64,72,80,88},{96,104,112,120},{128,136,144,1..., dimensions={0} | all-to-all | bytes 557056 | tf_op jit(solution)/shard_map/all_to_all | solution.py:267
  90.7 3.2 %collective-permute-done.6 = f32[136,128]{1,0:T(8,128)S(1)} collective-permute-done((f32[136,128]{1,0:T(8,128)S(1)}, f32[136,128]{1,0:T(8,128)S(1)}, u32[]{:S(2)}, u32[]{:S(2)}) %collective-permute-start.6) | collective-permute-done | bytes 69664 | tf_op jit(solution)/shard_map/ppermute | solution.py:271
  93.9 3.3 %collective-permute-start.7 = (f32[136,128]{1,0:T(8,128)S(1)}, f32[136,128]{1,0:T(8,128)S(1)}, u32[]{:S(2)}, u32[]{:S(2)}) collective-permute-start(f32[136,128]{1,0:T(8,128)S(1)} %add.21), channel_id=1, source_target_pairs={{0,64},{8,72},{16,80},{24,88},{32,96},{40,104},{48,112},{56,120},{... | collective-permute-start | bytes 208904 | tf_op jit(solution)/shard_map/ppermute | solution.py:271
  97.2 3.8 %collective-permute-done.7 = f32[136,128]{1,0:T(8,128)S(1)} collective-permute-done((f32[136,128]{1,0:T(8,128)S(1)}, f32[136,128]{1,0:T(8,128)S(1)}, u32[]{:S(2)}, u32[]{:S(2)}) %collective-permute-start.7) | collective-permute-done | bytes 69664 | tf_op jit(solution)/shard_map/ppermute | solution.py:271
  101.1 6.4 %collective-permute-start.8 = (f32[136,128]{1,0:T(8,128)S(1)}, f32[136,128]{1,0:T(8,128)S(1)}, u32[]{:S(2)}, u32[]{:S(2)}) collective-permute-start(f32[136,128]{1,0:T(8,128)S(1)} %add.22), channel_id=1, source_target_pairs={{0,128},{8,136},{16,144},{24,152},{32,160},{40,168},{48,176},{56,1... | collective-permute-start | bytes 208904 | tf_op jit(solution)/shard_map/ppermute | solution.py:271
  107.5 2.3 %collective-permute-done.8 = f32[136,128]{1,0:T(8,128)S(1)} collective-permute-done((f32[136,128]{1,0:T(8,128)S(1)}, f32[136,128]{1,0:T(8,128)S(1)}, u32[]{:S(2)}, u32[]{:S(2)}) %collective-permute-start.8) | collective-permute-done | bytes 69664 | tf_op jit(solution)/shard_map/ppermute | solution.py:271
  109.8 15.7 %collective-permute-done.9 = f32[136,128]{1,0:T(8,128)S(1)} collective-permute-done((f32[136,128]{1,0:T(8,128)S(1)}, f32[136,128]{1,0:T(8,128)S(1)}, u32[]{:S(2)}, u32[]{:S(2)}) %collective-permute-start.9) | collective-permute-done | bytes 69664 | tf_op jit(solution)/shard_map/ppermute | solution.py:273
  125.6 10.6 %all_to_all.22.sums_ref = f32[4,2,136,128]{3,2,1,0:T(8,128)S(1)} all-to-all(f32[4,2,136,128]{3,2,1,0:T(8,128)S(1)} %broadcast_in_dim.7), channel_id=1, replica_groups={{0,8,16,24},{32,40,48,56},{64,72,80,88},{96,104,112,120},{128,136,144,1..., dimensions={0} | all-to-all | bytes 1114112 | tf_op jit(solution)/shard_map/all_to_all | solution.py:274
  136.2 11.9 %turn.3 = f32[1024,1024]{1,0:T(8,128)} custom-call(f32[4,2,136,128]{3,2,1,0:T(8,128)S(1)} %all_to_all.22.sums_ref, f32[1024,1024]{1,0:T(8,128)} %turn.2.x_ref.own_ref, f32[1024,1024]{1,0:T(8,128)} %collective-permute-done.10.prev_ref), custom_call_target="tpu_custom_call" | custom-call | tf_op jit(solution)/shard_map/turn/pallas_call | solution.py:252
  (25 shorter events, 3.0 us)
Async XLA Ops:
  0.0 63.5 %collective-permute-start.4 = (f32[1024,1024]{1,0:T(8,128)}, f32[1024,1024]{1,0:T(8,128)}, u32[]{:S(2)}, u32[]{:S(2)}) collective-permute-start(f32[1024,1024]{1,0:T(8,128)} %own_ref.1), channel_id=1, source_target_pairs={{0,1},{1,2},{2,3},{3,4},{4,5},{5,6},{6,7},{7,0},{8,9},{9,10},{10,1... | collective-permute-start | bytes 12582920 | tf_op jit(solution)/shard_map/ppermute | solution.py:284
  0.0 2.2 %copy-start = (f32[1024,1024]{1,0:T(8,128)S(1)}, f32[1024,1024]{1,0:T(8,128)}, u32[]{:S(2)}) copy-start(f32[1024,1024]{1,0:T(8,128)} %own_ref.1) | copy-start | bytes 12582916
  2.2 0.7 copy-start.1
  2.9 53.8 %copy-start.2 = (s32[2,1,8]{2,1,0:T(1,128)S(1)}, s32[2,1,8]{2,1,0:T(1,128)}, u32[]{:S(2)}) copy-start(s32[2,1,8]{2,1,0:T(1,128)} %refs_0_.3) | copy-start | bytes 196
  17.3 5.0 %collective-permute-start = (f32[136,128]{1,0:T(8,128)S(1)}, f32[136,128]{1,0:T(8,128)S(1)}, u32[]{:S(2)}, u32[]{:S(2)}) collective-permute-start(f32[136,128]{1,0:T(8,128)S(1)} %reduce_sum.18), channel_id=1, source_target_pairs={{0,32},{8,40},{16,48},{24,56},{32,0},{40,8},{48,16},{56,24},{64,96... | collective-permute-start | bytes 208904 | tf_op jit(solution)/shard_map/ppermute | solution.py:271
  22.2 7.2 %collective-permute-start.1 = (f32[136,128]{1,0:T(8,128)S(1)}, f32[136,128]{1,0:T(8,128)S(1)}, u32[]{:S(2)}, u32[]{:S(2)}) collective-permute-start(f32[136,128]{1,0:T(8,128)S(1)} %add.18), channel_id=1, source_target_pairs={{0,64},{8,72},{16,80},{24,88},{32,96},{40,104},{48,112},{56,120},{... | collective-permute-start | bytes 208904 | tf_op jit(solution)/shard_map/ppermute | solution.py:271
  29.5 8.7 %collective-permute-start.2 = (f32[136,128]{1,0:T(8,128)S(1)}, f32[136,128]{1,0:T(8,128)S(1)}, u32[]{:S(2)}, u32[]{:S(2)}) collective-permute-start(f32[136,128]{1,0:T(8,128)S(1)} %add.19), channel_id=1, source_target_pairs={{0,128},{8,136},{16,144},{24,152},{32,160},{40,168},{48,176},{56,1... | collective-permute-start | bytes 208904 | tf_op jit(solution)/shard_map/ppermute | solution.py:271
  38.2 11.9 %collective-permute-start.3 = (f32[136,128]{1,0:T(8,128)S(1)}, f32[136,128]{1,0:T(8,128)S(1)}, u32[]{:S(2)}, u32[]{:S(2)}) collective-permute-start(f32[136,128]{1,0:T(8,128)S(1)} %add.20), channel_id=1, source_target_pairs={{0,1},{1,2},{2,3},{3,4},{4,5},{5,6},{6,7},{7,0},{8,9},{9,10},{10,1... | collective-permute-start | bytes 208904 | tf_op jit(solution)/shard_map/ppermute | solution.py:273
  51.0 12.5 %all-to-all-start.1 = ((f32[4,2,136,128]{3,2,1,0:T(8,128)}), f32[4,2,136,128]{3,2,1,0:T(8,128)S(1)}, u32[]{:S(2)}, u32[]{:S(2)}) async-start(f32[4,2,136,128]{3,2,1,0:T(8,128)} %broadcast_in_dim.6), calls=%async_computation.1 | async-start | bytes 1114112 | tf_op jit(solution)/shard_map/all_to_all | solution.py:274
  56.7 4.2 %collective-permute-start.5 = (s32[2,1,8]{2,1,0:T(1,128)S(1)}, s32[2,1,8]{2,1,0:T(1,128)S(1)}, u32[]{:S(2)}, u32[]{:S(2)}) collective-permute-start(s32[2,1,8]{2,1,0:T(1,128)S(1)} %copy-done.2), channel_id=1, source_target_pairs={{0,1},{1,2},{2,3},{3,4},{4,5},{5,6},{6,7},{7,0},{8,9},{9,10},{10,1... | collective-permute-start | bytes 200 | tf_op jit(solution)/shard_map/ppermute | solution.py:281
  75.4 60.8 %collective-permute-start.10 = (f32[1024,1024]{1,0:T(8,128)}, f32[1024,1024]{1,0:T(8,128)}, u32[]{:S(2)}, u32[]{:S(2)}) collective-permute-start(f32[1024,1024]{1,0:T(8,128)} %turn.2.x_ref.own_ref), channel_id=1, source_target_pairs={{0,1},{1,2},{2,3},{3,4},{4,5},{5,6},{6,7},{7,0},{8,9},{9,10},{10,1... | collective-permute-start | bytes 12582920 | tf_op jit(solution)/shard_map/ppermute | solution.py:284
  89.5 4.4 %collective-permute-start.6 = (f32[136,128]{1,0:T(8,128)S(1)}, f32[136,128]{1,0:T(8,128)S(1)}, u32[]{:S(2)}, u32[]{:S(2)}) collective-permute-start(f32[136,128]{1,0:T(8,128)S(1)} %reduce_sum.19), channel_id=1, source_target_pairs={{0,32},{8,40},{16,48},{24,56},{32,0},{40,8},{48,16},{56,24},{64,96... | collective-permute-start | bytes 208904 | tf_op jit(solution)/shard_map/ppermute | solution.py:271
  93.9 7.2 %collective-permute-start.7 = (f32[136,128]{1,0:T(8,128)S(1)}, f32[136,128]{1,0:T(8,128)S(1)}, u32[]{:S(2)}, u32[]{:S(2)}) collective-permute-start(f32[136,128]{1,0:T(8,128)S(1)} %add.21), channel_id=1, source_target_pairs={{0,64},{8,72},{16,80},{24,88},{32,96},{40,104},{48,112},{56,120},{... | collective-permute-start | bytes 208904 | tf_op jit(solution)/shard_map/ppermute | solution.py:271
  101.1 8.7 %collective-permute-start.8 = (f32[136,128]{1,0:T(8,128)S(1)}, f32[136,128]{1,0:T(8,128)S(1)}, u32[]{:S(2)}, u32[]{:S(2)}) collective-permute-start(f32[136,128]{1,0:T(8,128)S(1)} %add.22), channel_id=1, source_target_pairs={{0,128},{8,136},{16,144},{24,152},{32,160},{40,168},{48,176},{56,1... | collective-permute-start | bytes 208904 | tf_op jit(solution)/shard_map/ppermute | solution.py:271
  109.8 15.7 %collective-permute-start.9 = (f32[136,128]{1,0:T(8,128)S(1)}, f32[136,128]{1,0:T(8,128)S(1)}, u32[]{:S(2)}, u32[]{:S(2)}) collective-permute-start(f32[136,128]{1,0:T(8,128)S(1)} %add.23), channel_id=1, source_target_pairs={{0,1},{1,2},{2,3},{3,4},{4,5},{5,6},{6,7},{7,0},{8,9},{9,10},{10,1... | collective-permute-start | bytes 208904 | tf_op jit(solution)/shard_map/ppermute | solution.py:273

commit v3 on v2

--- a/solution.py
+++ b/solution.py
@@ -10,6 +10,7 @@
 WIDTH = 128
 PAIRS = 4
 PLACES = 2 * PAIRS
+EARLY = 5
 PANEL = 32
 PACK = WIDTH // PANEL
 SUB = 8
@@ -24,33 +25,26 @@
     return high, (value - high.astype(jnp.float32)).astype(jnp.bfloat16)
 
 
-def load_blocks(source, held, sems):
-    for place in range(PLACES):
-        pltpu.make_async_copy(source.at[:, pl.ds(place * WIDTH, WIDTH)], held.at[place], sems.at[place]).start()
-
-
-def wait_block(source, held, sems, place):
-    pltpu.make_async_copy(source.at[:, pl.ds(0, WIDTH)], held.at[place], sems.at[place]).wait()
-
-
-def gram_kernel(step, x_ref, *refs):
-    if step is None:
-        out_ref, held, sems = refs
-        load_blocks(x_ref, held, sems)
-        order = list(range(PLACES))
-    else:
-        plan_ref, out_ref, held, sems, plan, plan_sem = refs
-        load_plan = pltpu.make_async_copy(plan_ref, plan, plan_sem)
-        load_plan.start()
-        load_blocks(x_ref, held, sems)
-        load_plan.wait()
-        order = [plan[step, 0, place] for place in range(PLACES)]
+def blocks_of(arrays):
+    return [
+        array.at[:, pl.ds(start, WIDTH)] for array in arrays for start in range(0, array.shape[1], WIDTH)
+    ]
+
+
+def load_blocks(arrays, held, sems):
+    for place, block in enumerate(blocks_of(arrays)):
+        pltpu.make_async_copy(block, held.at[place], sems.at[place]).start()
+
+
+def wait_blocks(arrays, held, sems):
+    for place, block in enumerate(blocks_of(arrays)):
+        pltpu.make_async_copy(block, held.at[place], sems.at[place]).wait()
+
+
+def gram_blocks(held, order, out_ref):
     line = lax.broadcasted_iota(jnp.int32, (8, WIDTH), 0)
     for pair in range(PAIRS):
-        both = order[2 * pair : 2 * pair + 2]
-        for place in both:
-            wait_block(x_ref, held, sems, place)
-        first, second = held[both[0]], held[both[1]]
+        first, second = held[order[2 * pair]], held[order[2 * pair + 1]]
         out_ref[pair, :WIDTH, :] = lax.dot_general(
             first, second, (((0,), (0,)), ((), ())), precision=HP, preferred_element_type=jnp.float32
         )
@@ -59,20 +53,68 @@
         out_ref[pair, WIDTH:, :] = jnp.where(line == 0, norm_first, jnp.where(line == 1, norm_second, 0.0))
 
 
-def gram(x, plan, step):
-    planned = step is not None
-    scratch = [pltpu.VMEM((PLACES, x.shape[0], WIDTH), jnp.float32), pltpu.SemaphoreType.DMA((PLACES,))]
-    if planned:
-        scratch += [pltpu.SMEM(plan.shape, jnp.int32), pltpu.SemaphoreType.DMA]
+def first_gram_kernel(plan_ref, x_ref, out_ref, early_ref, late_ref, held, sems, out_sems, plan, plan_sem):
+    load_plan = pltpu.make_async_copy(plan_ref, plan, plan_sem)
+    load_plan.start()
+    load_blocks((x_ref,), held, sems)
+    wait_blocks((x_ref,), held, sems)
+    copies = [
+        pltpu.make_async_copy(held.at[place], block, out_sems.at[place])
+        for place, block in enumerate(blocks_of((early_ref, late_ref)))
+    ]
+    for copy in copies:
+        copy.start()
+    load_plan.wait()
+    gram_blocks(held, [plan[0, 0, place] for place in range(PLACES)], out_ref)
+    for copy in copies:
+        copy.wait()
+
+
+def later_gram_kernel(early_ref, late_ref, out_ref, held, sems):
+    load_blocks((early_ref, late_ref), held, sems)
+    wait_blocks((early_ref, late_ref), held, sems)
+    gram_blocks(held, range(PLACES), out_ref)
+
+
+SUMS = jax.ShapeDtypeStruct((PAIRS, GROUP_ROWS, WIDTH), jnp.float32)
+
+
+def pieces(height):
+    return tuple(jax.ShapeDtypeStruct((height, count * WIDTH), jnp.float32) for count in (EARLY, PLACES - EARLY))
+
+
+def first_gram(x, plan):
+    height = x.shape[0]
     return pl.pallas_call(
-        functools.partial(gram_kernel, step),
-        out_shape=jax.ShapeDtypeStruct((PAIRS, GROUP_ROWS, WIDTH), jnp.float32),
-        in_specs=[pl.BlockSpec(memory_space=pl.ANY)] * (2 if planned else 1),
+        first_gram_kernel,
+        out_shape=(SUMS,) + pieces(height),
+        in_specs=[pl.BlockSpec(memory_space=pl.ANY), pl.BlockSpec(memory_space=pltpu.HBM)],
+        out_specs=[pl.BlockSpec(memory_space=pltpu.VMEM)] + [pl.BlockSpec(memory_space=pltpu.HBM)] * 2,
+        scratch_shapes=[
+            pltpu.VMEM((PLACES, height, WIDTH), jnp.float32),
+            pltpu.SemaphoreType.DMA((PLACES,)),
+            pltpu.SemaphoreType.DMA((PLACES,)),
+            pltpu.SMEM(plan.shape, jnp.int32),
+            pltpu.SemaphoreType.DMA,
+        ],
+        compiler_params=PARAMS,
+        name="first_gram",
+    )(plan, x)
+
+
+def later_gram(early, late):
+    return pl.pallas_call(
+        later_gram_kernel,
+        out_shape=SUMS,
+        in_specs=[pl.BlockSpec(memory_space=pltpu.HBM)] * 2,
         out_specs=pl.BlockSpec(memory_space=pltpu.VMEM),
-        scratch_shapes=scratch,
+        scratch_shapes=[
+            pltpu.VMEM((PLACES, early.shape[0], WIDTH), jnp.float32),
+            pltpu.SemaphoreType.DMA((PLACES,)),
+        ],
         compiler_params=PARAMS,
-        name="gram",
-    )(*((x, plan) if planned else (x,)))
+        name="later_gram",
+    )(early, late)
 
 
 def panel_inverse(block):
@@ -183,20 +225,7 @@
     return [(halves[pair][0], systems[pair][:, :width], systems[pair][:, width:]) for pair in range(count)]
 
 
-def turn_kernel(step, sums_ref, own_ref, prev_ref, *refs):
-    if step is None:
-        out_ref, held, sides, turned, in_sems, out_sems = refs
-        plans = []
-    else:
-        own_plan_ref, prev_plan_ref, out_ref, held, sides, turned, in_sems, out_sems, plan, plan_sems = refs
-        plans = [
-            pltpu.make_async_copy(ref, plan.at[which], plan_sems.at[which])
-            for which, ref in enumerate((own_plan_ref, prev_plan_ref))
-        ]
-        for copy in plans:
-            copy.start()
-    for which, ref in enumerate((own_ref, prev_ref)):
-        load_blocks(ref, held.at[which], in_sems.at[which])
+def rotate_kernel(sums_ref, sides_ref):
     width = WIDTH
     row = lax.broadcasted_iota(jnp.int32, (width, width), 0)
     lane = lax.broadcasted_iota(jnp.int32, (width, width), 1)
@@ -207,60 +236,92 @@
             top, bottom = 2.0 * inverse - eye, -2.0 * across.T
         else:
             top, bottom = 2.0 * across, eye - 2.0 * square_dot(split3(half), split3(across), 0)
-        high, low = split(jnp.concatenate([top, bottom], axis=0))
-        sides[index, :, :width] = high
-        sides[index, :, width:] = low
+        for start, part in ((0, top), (width, bottom)):
+            high, low = split(part)
+            sides_ref[index, start : start + width, :width] = high
+            sides_ref[index, start : start + width, width:] = low
+
+
+def rotate(sums):
+    return pl.pallas_call(
+        rotate_kernel,
+        out_shape=jax.ShapeDtypeStruct((2 * PAIRS, 2 * WIDTH, 2 * WIDTH), jnp.bfloat16),
+        in_specs=[pl.BlockSpec(memory_space=pltpu.VMEM)],
+        out_specs=pl.BlockSpec(memory_space=pltpu.VMEM),
+        compiler_params=PARAMS,
+        name="rotate",
+    )(sums)
+
+
+def turn_kernel(last, sides_ref, early_ref, late_ref, prev_early_ref, prev_late_ref, *refs):
+    if last:
+        out_ref, held, turned, in_sems, out_sems = refs
+        outs = (out_ref,)
+        plans = []
+    else:
+        own_plan_ref, prev_plan_ref, *outs, held, turned, in_sems, out_sems, plan, plan_sems = refs
+        plans = [
+            pltpu.make_async_copy(ref, plan.at[which], plan_sems.at[which])
+            for which, ref in enumerate((own_plan_ref, prev_plan_ref))
+        ]
+        for copy in plans:
+            copy.start()
+    sources = [blocks_of(arrays) for arrays in ((early_ref, late_ref), (prev_early_ref, prev_late_ref))]
+    for place in range(PLACES):
+        for which in range(2):
+            pltpu.make_async_copy(sources[which][place], held.at[which, place], in_sems.at[which, place]).start()
     for copy in plans:
         copy.wait()
-    for which, ref in enumerate((own_ref, prev_ref)):
-        for place in range(PLACES):
-            wait_block(ref, held.at[which], in_sems.at[which], place)
+    width = WIDTH
     copies = []
-    for slot in range(PLACES):
-        if step is None:
+    for slot, target in enumerate(blocks_of(outs)):
+        if last:
             which, pair = slot % 2, slot // 2
-            first, second = 2 * pair, 2 * pair + 1
+            both = (2 * pair, 2 * pair + 1)
         else:
-            place = plan[0, step + 1, 0, slot]
+            place = plan[0, 1, 0, slot]
             which, pair = place % 2, place // 2
-            first, second = plan[which, step, 0, 2 * pair], plan[which, step, 0, 2 * pair + 1]
-        high, low = split(jnp.concatenate([held[which, first], held[which, second]], axis=1))
-        side = sides[which * PAIRS + pair]
+            both = (plan[which, 0, 0, 2 * pair], plan[which, 0, 0, 2 * pair + 1])
+        for place in both:
+            pltpu.make_async_copy(sources[0][0], held.at[which, place], in_sems.at[which, place]).wait()
+        high, low = split(jnp.concatenate([held[which, place] for place in both], axis=1))
+        side = sides_ref[which * PAIRS + pair]
         parts = jnp.dot(high, side, preferred_element_type=jnp.float32)
         rest = jnp.dot(low, side[:, :width], preferred_element_type=jnp.float32)
         turned[slot] = parts[:, :width] + (parts[:, width:] + rest)
-        copies.append(
-            pltpu.make_async_copy(turned.at[slot], out_ref.at[:, pl.ds(slot * width, width)], out_sems.at[slot])
-        )
+        copies.append(pltpu.make_async_copy(turned.at[slot], target, out_sems.at[slot]))
         copies[-1].start()
     for copy in copies:
         copy.wait()
 
 
-def turn(sums, own, prev, own_plan, prev_plan, step):
-    planned = step is not None
-    height = own.shape[0]
+def turn(sides, own, prev, plans):
+    height = own[0].shape[0]
     scratch = [
         pltpu.VMEM((2, PLACES, height, WIDTH), jnp.float32),
-        pltpu.VMEM((2 * PAIRS, 2 * WIDTH, 2 * WIDTH), jnp.bfloat16),
         pltpu.VMEM((PLACES, height, WIDTH), jnp.float32),
         pltpu.SemaphoreType.DMA((2, PLACES)),
         pltpu.SemaphoreType.DMA((PLACES,)),
     ]
-    if planned:
-        scratch += [pltpu.SMEM((2,) + own_plan.shape, jnp.int32), pltpu.SemaphoreType.DMA((2,))]
+    if plans:
+        scratch += [pltpu.SMEM((2,) + plans[0].shape, jnp.int32), pltpu.SemaphoreType.DMA((2,))]
+        shapes = pieces(height)
+    else:
+        shapes = (jax.ShapeDtypeStruct((height, PLACES * WIDTH), jnp.float32),)
     return pl.pallas_call(
-        functools.partial(turn_kernel, step),
-        out_shape=jax.ShapeDtypeStruct(own.shape, jnp.float32),
-        in_specs=[pl.BlockSpec(memory_space=pltpu.VMEM)] + [pl.BlockSpec(memory_space=pl.ANY)] * (4 if planned else 2),
-        out_specs=pl.BlockSpec(memory_space=pl.ANY),
+        functools.partial(turn_kernel, not plans),
+        out_shape=shapes,
+        in_specs=[pl.BlockSpec(memory_space=pltpu.VMEM)]
+        + [pl.BlockSpec(memory_space=pltpu.HBM)] * 4
+        + [pl.BlockSpec(memory_space=pl.ANY)] * len(plans),
+        out_specs=[pl.BlockSpec(memory_space=pltpu.HBM)] * len(shapes),
         scratch_shapes=scratch,
         compiler_params=PARAMS,
         name="turn",
-    )(sums, own, prev, *((own_plan, prev_plan) if planned else ()))
-
-
-def summed(parts, onward):
+    )(sides, *own, *prev, *plans)
+
+
+def summed(parts, late, extra):
     nx, count = PAIRS, lax.axis_size("rows")
     nz = count // nx
     beside = [[z * nx + x for x in range(nx)] for z in range(nz)]
@@ -268,23 +329,29 @@
     mine = jnp.sum(parts, axis=0)
     step = 1
     while step < nz:
-        mine = mine + lax.ppermute(mine, "rows", [(i, (((i // nx) ^ step) * nx) + i % nx) for i in range(count)])
+        turned = nz - 1 if 2 * step == nz else step
+        mine = mine + lax.ppermute(mine, "rows", [(i, (((i // nx) ^ turned) * nx) + i % nx) for i in range(count)])
         step *= 2
-    both = jnp.stack([mine, lax.ppermute(mine, "pairs", onward)])
-    return lax.all_to_all(jnp.broadcast_to(both, (nx,) + both.shape), "rows", 0, 0, axis_index_groups=beside)
+    theirs, extra, late = lax.optimization_barrier((onward(mine), onward(extra) if extra is not None else (), late))
+    late = onward(late)
+    both = jnp.stack([mine, theirs])
+    both = lax.all_to_all(jnp.broadcast_to(both, (nx,) + both.shape), "rows", 0, 0, axis_index_groups=beside)
+    return both, late, extra
+
+
+def onward(value):
+    count = lax.axis_size("pairs")
+    return lax.ppermute(value, "pairs", [(q, (q + 1) % count) for q in range(count)])
 
 
 def local(snapshot, plan):
-    count = lax.axis_size("pairs")
-    onward = [(q, (q + 1) % count) for q in range(count)]
-    steps = plan.shape[0]
-    prev_plan = lax.ppermute(plan, "pairs", onward)
-    x = snapshot
-    for step in range(steps):
-        prev = lax.ppermute(x, "pairs", onward)
-        sums = summed(gram(x, plan, step if step == 0 else None), onward)
-        x = turn(sums, x, prev, plan, prev_plan, step if step == 0 else None)
-    return x
+    parts, early, late = first_gram(snapshot, plan)
+    prev_early = onward(early)
+    sums, prev_late, prev_plan = summed(parts, late, plan)
+    early, late = turn(rotate(sums), (early, late), (prev_early, prev_late), (plan, prev_plan))
+    prev_early = onward(early)
+    sums, prev_late, _ = summed(later_gram(early, late), late, None)
+    return turn(rotate(sums), (early, late), (prev_early, prev_late), ())[0]
 
 
 def solution(mesh):

time: 149 us -> 133 us (0.89)
  waiting for transfers between devices: 52.9 us -> 34 us
  blocking collectives: 31.8 us -> 45.2 us
  starting transfers between devices: 28.4 us -> 17.1 us
  Pallas kernels: 31 us -> 32.5 us
    ppermute x11 -> x13, waiting for transfers between devices: 50.3 us -> 34 us  [the longest x6 20.9 us: summed(): lax.ppermute(mine, 'rows', [(i, (i // nx ^ turned) * nx + i % nx) for i i...]
    all_to_all x1 -> x2, blocking collectives: 10.6 us -> 25.1 us  [summed(): lax.all_to_all(jnp.broadcast_to(both, (nx,) + both.shape), 'rows', 0, 0,...]
    all_to_all x1 -> x0, starting transfers between devices: 5.71 us -> none  [summed(): lax.all_to_all(jnp.broadcast_to(both, (nx,) + both.shape), 'rows', 0, 0,...]
    ppermute x11 -> x13, starting transfers between devices: 22.7 us -> 17.1 us  [the longest x6 16.1 us: summed(): lax.ppermute(mine, 'rows', [(i, (i // nx ^ turned) * nx + i % nx) for i i...]
    all_to_all x1 -> x0, waiting for transfers between devices: 2.6 us -> none  [summed(): lax.all_to_all(jnp.broadcast_to(both, (nx,) + both.shape), 'rows', 0, 0,...]
    pallas_call x4 -> x6, Pallas kernels: 31 us -> 32.5 us  [the longest x2 13 us: rotate(): pl.pallas_call(rotate_kernel, out_shape=jax.ShapeDtypeStruct((2 * PAIRS,...]
    unnamed x6 -> x12, local copies, waits for them, and re-layouts: 2.87 us -> 3.58 us
  transfers between devices with their start and end apart: 12 -> 13, of which waited for: 10 -> 10; matrix products, arithmetic and copies ran while one was open for 1% -> 0% of each run, Pallas kernels for 5% -> 12%
where the time goes in v3:
time: 133 us
  blocking collectives  45.2 us (34%)
  waiting for transfers between devices  34 us (26%)
  Pallas kernels  32.5 us (24%)
  starting transfers between devices  17.1 us (13%)
  local copies, waits for them, and re-layouts  3.65 us (3%)
    all_to_all x2, blocking collectives, summed(): lax.all_to_all(jnp.broadcast_to(both, (nx,) + both.shape), 'rows', 0, 0,...  25.1 us
    ppermute x6, waiting for transfers between devices, summed(): lax.ppermute(mine, 'rows', [(i, (i // nx ^ turned) * nx + i % nx) for i i...  20.9 us
    all_to_all x2, blocking collectives, summed(): parts = lax.all_to_all(parts, 'rows', 0, 0, axis_index_groups=beside)  20.1 us
    ppermute x6, starting transfers between devices, summed(): lax.ppermute(mine, 'rows', [(i, (i // nx ^ turned) * nx + i % nx) for i i...  16.1 us
    ppermute x7, waiting for transfers between devices, onward(): lax.ppermute(value, 'pairs', [(q, (q + 1) % count) for q in range(count)])  13.1 us
    pallas_call x2, Pallas kernels, rotate(): pl.pallas_call(rotate_kernel, out_shape=jax.ShapeDtypeStruct((2 * PAIRS,...  13 us
    pallas_call x2, Pallas kernels, turn(): pl.pallas_call(functools.partial(turn_kernel, not plans), out_shape=shape...  12.2 us
    pallas_call x1, Pallas kernels, first_gram(): pl.pallas_call(first_gram_kernel, out_shape=(SUMS,) + pieces(height), in_...  4.71 us
  transfers between devices with their start and end apart: 13, of which 10 were waited for; matrix products, arithmetic and copies ran while one was open for 0% of the time, Pallas kernels for 12%

profile of v3, /device:TPU:2, one launch (start us, length us, event | category | flops | bytes accessed | tf_op | source)
XLA Modules:
  0.0 132.9 jit_solution(10262987435408444417)
XLA Ops:
  0.7 4.7 %first_gram.1 = (f32[4,136,128]{2,1,0:T(8,128)S(1)}, f32[1024,640]{1,0:T(8,128)S(1)}, f32[1024,384]{1,0:T(8,128)S(1)}) custom-call(s32[2,1,8]{2,1,0:T(1,128)S(1)} %copy-done.4, f32[1024,1024]{1,0:T(8,128)} %x_ref.1), custom_call_target="tpu_custom_call" | custom-call | tf_op jit(solution)/shard_map/first_gram/pallas_call | solution.py:88
  6.6 11.1 %all_to_all.20 = f32[4,136,128]{2,1,0:T(8,128)S(1)} all-to-all(f32[4,136,128]{2,1,0:T(8,128)S(1)} %get-tuple-element.15), channel_id=1, replica_groups={{0,8,16,24},{32,40,48,56},{64,72,80,88},{96,104,112,120},{128,136,144,1..., dimensions={0} | all-to-all | bytes 557056 | tf_op jit(solution)/shard_map/all_to_all | solution.py:328
  17.7 2.0 %collective-permute-start = (f32[136,128]{1,0:T(8,128)S(1)}, f32[136,128]{1,0:T(8,128)S(1)}, u32[]{:S(2)}, u32[]{:S(2)}) collective-permute-start(f32[136,128]{1,0:T(8,128)S(1)} %reduce_sum.18), channel_id=1, source_target_pairs={{0,32},{8,40},{16,48},{24,56},{32,0},{40,8},{48,16},{56,24},{64,96... | collective-permute-start | bytes 208904 | tf_op jit(solution)/shard_map/ppermute | solution.py:333
  19.6 2.9 %collective-permute-done = f32[136,128]{1,0:T(8,128)S(1)} collective-permute-done((f32[136,128]{1,0:T(8,128)S(1)}, f32[136,128]{1,0:T(8,128)S(1)}, u32[]{:S(2)}, u32[]{:S(2)}) %collective-permute-start) | collective-permute-done | bytes 69664 | tf_op jit(solution)/shard_map/ppermute | solution.py:333
  22.6 3.4 %collective-permute-start.1 = (f32[136,128]{1,0:T(8,128)S(1)}, f32[136,128]{1,0:T(8,128)S(1)}, u32[]{:S(2)}, u32[]{:S(2)}) collective-permute-start(f32[136,128]{1,0:T(8,128)S(1)} %add.18), channel_id=1, source_target_pairs={{0,64},{8,72},{16,80},{24,88},{32,96},{40,104},{48,112},{56,120},{... | collective-permute-start | bytes 208904 | tf_op jit(solution)/shard_map/ppermute | solution.py:333
  26.0 3.8 %collective-permute-done.1 = f32[136,128]{1,0:T(8,128)S(1)} collective-permute-done((f32[136,128]{1,0:T(8,128)S(1)}, f32[136,128]{1,0:T(8,128)S(1)}, u32[]{:S(2)}, u32[]{:S(2)}) %collective-permute-start.1) | collective-permute-done | bytes 69664 | tf_op jit(solution)/shard_map/ppermute | solution.py:333
  29.8 5.0 %collective-permute-start.2 = (f32[136,128]{1,0:T(8,128)S(1)}, f32[136,128]{1,0:T(8,128)S(1)}, u32[]{:S(2)}, u32[]{:S(2)}) collective-permute-start(f32[136,128]{1,0:T(8,128)S(1)} %add.19), channel_id=1, source_target_pairs={{0,224},{8,232},{16,240},{24,248},{32,192},{40,200},{48,208},{56,2... | collective-permute-start | bytes 208904 | tf_op jit(solution)/shard_map/ppermute | solution.py:333
  34.9 2.8 %collective-permute-done.2 = f32[136,128]{1,0:T(8,128)S(1)} collective-permute-done((f32[136,128]{1,0:T(8,128)S(1)}, f32[136,128]{1,0:T(8,128)S(1)}, u32[]{:S(2)}, u32[]{:S(2)}) %collective-permute-start.2) | collective-permute-done | bytes 69664 | tf_op jit(solution)/shard_map/ppermute | solution.py:333
  38.6 4.0 %collective-permute-done.4.refs_1_ = s32[2,1,8]{2,1,0:T(1,128)S(1)} collective-permute-done((s32[2,1,8]{2,1,0:T(1,128)S(1)}, s32[2,1,8]{2,1,0:T(1,128)S(1)}, u32[]{:S(2)}, u32[]{:S(2)}) %collective-permute-start.4) | collective-permute-done | bytes 96 | tf_op jit(solution)/shard_map/ppermute | solution.py:344
  42.7 12.8 %all_to_all.21.sums_ref = f32[4,2,136,128]{3,2,1,0:T(8,128)S(1)} all-to-all(f32[4,2,136,128]{3,2,1,0:T(8,128)S(1)} %broadcast_in_dim.6), channel_id=1, replica_groups={{0,8,16,24},{32,40,48,56},{64,72,80,88},{96,104,112,120},{128,136,144,1..., dimensions={0} | all-to-all | bytes 1114112 | tf_op jit(solution)/shard_map/all_to_all | solution.py:338
  55.5 6.5 %rotate.2.sides_ref = bf16[8,256,256]{2,1,0:T(8,128)(2,1)S(1)} custom-call(f32[4,2,136,128]{3,2,1,0:T(8,128)S(1)} %all_to_all.21.sums_ref), custom_call_target="tpu_custom_call" | custom-call | tf_op jit(solution)/shard_map/rotate/pallas_call | solution.py:246
  62.0 1.9 %collective-permute-done.6.prev_late_ref = f32[1024,384]{1,0:T(8,128)S(1)} collective-permute-done((f32[1024,384]{1,0:T(8,128)}, f32[1024,384]{1,0:T(8,128)S(1)}, u32[]{:S(2)}, u32[]{:S(2)}) %collective-permute-start.6) | collective-permute-done | bytes 1572896 | tf_op jit(solution)/shard_map/ppermute | solution.py:344
  63.9 6.2 %turn.2 = (f32[1024,640]{1,0:T(8,128)}, f32[1024,384]{1,0:T(8,128)S(1)}) custom-call(bf16[8,256,256]{2,1,0:T(8,128)(2,1)S(1)} %rotate.2.sides_ref, f32[1024,640]{1,0:T(8,128)} %copy-done.1, f32[1024,384]{1,0:T(8,128)S(1)} %copy-done.3, f32[1024,640]{1,0:T(8,128)} %collective-permute-done.5.prev_early_ref, ...), custom_call_target="tpu_custom_call" | custom-call | tf_op jit(solution)/shard_map/turn/pallas_call | solution.py:311
  71.9 2.6 %later_gram.1 = f32[4,136,128]{2,1,0:T(8,128)S(1)} custom-call(f32[1024,640]{1,0:T(8,128)S(1)} %copy-done, f32[1024,384]{1,0:T(8,128)S(1)} %get-tuple-element.24.late_ref), custom_call_target="tpu_custom_call" | custom-call | tf_op jit(solution)/shard_map/later_gram/pallas_call | solution.py:106
  74.5 9.0 %all_to_all.22 = f32[4,136,128]{2,1,0:T(8,128)S(1)} all-to-all(f32[4,136,128]{2,1,0:T(8,128)S(1)} %later_gram.1), channel_id=1, replica_groups={{0,8,16,24},{32,40,48,56},{64,72,80,88},{96,104,112,120},{128,136,144,1..., dimensions={0} | all-to-all | bytes 557056 | tf_op jit(solution)/shard_map/all_to_all | solution.py:328
  84.0 4.0 %collective-permute-done.7 = f32[136,128]{1,0:T(8,128)S(1)} collective-permute-done((f32[136,128]{1,0:T(8,128)S(1)}, f32[136,128]{1,0:T(8,128)S(1)}, u32[]{:S(2)}, u32[]{:S(2)}) %collective-permute-start.7) | collective-permute-done | bytes 69664 | tf_op jit(solution)/shard_map/ppermute | solution.py:333
  89.3 4.5 %collective-permute-done.8 = f32[136,128]{1,0:T(8,128)S(1)} collective-permute-done((f32[136,128]{1,0:T(8,128)S(1)}, f32[136,128]{1,0:T(8,128)S(1)}, u32[]{:S(2)}, u32[]{:S(2)}) %collective-permute-start.8) | collective-permute-done | bytes 69664 | tf_op jit(solution)/shard_map/ppermute | solution.py:333
  93.8 4.1 %collective-permute-start.9 = (f32[136,128]{1,0:T(8,128)S(1)}, f32[136,128]{1,0:T(8,128)S(1)}, u32[]{:S(2)}, u32[]{:S(2)}) collective-permute-start(f32[136,128]{1,0:T(8,128)S(1)} %add.22), channel_id=1, source_target_pairs={{0,224},{8,232},{16,240},{24,248},{32,192},{40,200},{48,208},{56,2... | collective-permute-start | bytes 208904 | tf_op jit(solution)/shard_map/ppermute | solution.py:333
  97.9 2.8 %collective-permute-done.9 = f32[136,128]{1,0:T(8,128)S(1)} collective-permute-done((f32[136,128]{1,0:T(8,128)S(1)}, f32[136,128]{1,0:T(8,128)S(1)}, u32[]{:S(2)}, u32[]{:S(2)}) %collective-permute-start.9) | collective-permute-done | bytes 69664 | tf_op jit(solution)/shard_map/ppermute | solution.py:333
  100.8 4.9 %collective-permute-done.10 = f32[136,128]{1,0:T(8,128)S(1)} collective-permute-done((f32[136,128]{1,0:T(8,128)S(1)}, f32[136,128]{1,0:T(8,128)S(1)}, u32[]{:S(2)}, u32[]{:S(2)}) %collective-permute-start.10) | collective-permute-done | bytes 69664 | tf_op jit(solution)/shard_map/ppermute | solution.py:344
  105.8 12.3 %all_to_all.23.sums_ref = f32[4,2,136,128]{3,2,1,0:T(8,128)S(1)} all-to-all(f32[4,2,136,128]{3,2,1,0:T(8,128)S(1)} %broadcast_in_dim.7), channel_id=1, replica_groups={{0,8,16,24},{32,40,48,56},{64,72,80,88},{96,104,112,120},{128,136,144,1..., dimensions={0} | all-to-all | bytes 1114112 | tf_op jit(solution)/shard_map/all_to_all | solution.py:338
  118.1 6.5 %rotate.3.sides_ref = bf16[8,256,256]{2,1,0:T(8,128)(2,1)S(1)} custom-call(f32[4,2,136,128]{3,2,1,0:T(8,128)S(1)} %all_to_all.23.sums_ref), custom_call_target="tpu_custom_call" | custom-call | tf_op jit(solution)/shard_map/rotate/pallas_call | solution.py:246
  124.6 2.2 %collective-permute-done.12.prev_late_ref = f32[1024,384]{1,0:T(8,128)S(1)} collective-permute-done((f32[1024,384]{1,0:T(8,128)S(1)}, f32[1024,384]{1,0:T(8,128)S(1)}, u32[]{:S(2)}, u32[]{:S(2)}) %collective-permute-start.12) | collective-permute-done | bytes 1572896 | tf_op jit(solution)/shard_map/ppermute | solution.py:344
  126.8 5.9 %turn.3 = f32[1024,1024]{1,0:T(8,128)} custom-call(bf16[8,256,256]{2,1,0:T(8,128)(2,1)S(1)} %rotate.3.sides_ref, f32[1024,640]{1,0:T(8,128)} %get-tuple-element.21.early_ref, f32[1024,384]{1,0:T(8,128)S(1)} %get-tuple-element.24.late_ref, f32[1024,640]{1,0:T(8,128)} %collective-permute-done.11.prev_early_ref, ...), custom_call_target="tpu_custom_call" | custom-call | tf_op jit(solution)/shard_map/turn/pallas_call | solution.py:311
  (36 shorter events, 6.5 us)
Async XLA Ops:
  0.0 0.7 copy-start.4
  0.7 37.0 %copy-start.5 = (s32[2,1,8]{2,1,0:T(1,128)S(1)}, s32[2,1,8]{2,1,0:T(1,128)}, u32[]{:S(2)}) copy-start(s32[2,1,8]{2,1,0:T(1,128)} %refs_0_.1) | copy-start | bytes 196
  5.4 1.2 copy-start.2
  6.6 57.4 %copy-start.1 = (f32[1024,640]{1,0:T(8,128)}, f32[1024,640]{1,0:T(8,128)S(1)}, u32[]{:S(2)}) copy-start(f32[1024,640]{1,0:T(8,128)S(1)} %get-tuple-element.18.early_ref) | copy-start | bytes 7864324
  6.6 57.4 %collective-permute-start.5 = (f32[1024,640]{1,0:T(8,128)S(1)}, f32[1024,640]{1,0:T(8,128)}, u32[]{:S(2)}, u32[]{:S(2)}) collective-permute-start(f32[1024,640]{1,0:T(8,128)S(1)} %get-tuple-element.18.early_ref), channel_id=1, source_target_pairs={{0,1},{1,2},{2,3},{3,4},{4,5},{5,6},{6,7},{7,0},{8,9},{9,10},{10,1... | collective-permute-start | bytes 7864328 | tf_op jit(solution)/shard_map/ppermute | solution.py:344
  17.6 46.3 %copy-start.3 = (f32[1024,384]{1,0:T(8,128)S(1)}, f32[1024,384]{1,0:T(8,128)}, u32[]{:S(2)}) copy-start(f32[1024,384]{1,0:T(8,128)} %copy-done.2) | copy-start | bytes 4718596
  17.7 4.9 %collective-permute-start = (f32[136,128]{1,0:T(8,128)S(1)}, f32[136,128]{1,0:T(8,128)S(1)}, u32[]{:S(2)}, u32[]{:S(2)}) collective-permute-start(f32[136,128]{1,0:T(8,128)S(1)} %reduce_sum.18), channel_id=1, source_target_pairs={{0,32},{8,40},{16,48},{24,56},{32,0},{40,8},{48,16},{56,24},{64,96... | collective-permute-start | bytes 208904 | tf_op jit(solution)/shard_map/ppermute | solution.py:333
  22.6 7.2 %collective-permute-start.1 = (f32[136,128]{1,0:T(8,128)S(1)}, f32[136,128]{1,0:T(8,128)S(1)}, u32[]{:S(2)}, u32[]{:S(2)}) collective-permute-start(f32[136,128]{1,0:T(8,128)S(1)} %add.18), channel_id=1, source_target_pairs={{0,64},{8,72},{16,80},{24,88},{32,96},{40,104},{48,112},{56,120},{... | collective-permute-start | bytes 208904 | tf_op jit(solution)/shard_map/ppermute | solution.py:333
  29.8 7.8 %collective-permute-start.2 = (f32[136,128]{1,0:T(8,128)S(1)}, f32[136,128]{1,0:T(8,128)S(1)}, u32[]{:S(2)}, u32[]{:S(2)}) collective-permute-start(f32[136,128]{1,0:T(8,128)S(1)} %add.19), channel_id=1, source_target_pairs={{0,224},{8,232},{16,240},{24,248},{32,192},{40,200},{48,208},{56,2... | collective-permute-start | bytes 208904 | tf_op jit(solution)/shard_map/ppermute | solution.py:333
  37.6 5.0 %collective-permute-start.3 = (f32[136,128]{1,0:T(8,128)S(1)}, f32[136,128]{1,0:T(8,128)S(1)}, u32[]{:S(2)}, u32[]{:S(2)}) collective-permute-start(f32[136,128]{1,0:T(8,128)S(1)} %add.20), channel_id=1, source_target_pairs={{0,1},{1,2},{2,3},{3,4},{4,5},{5,6},{6,7},{7,0},{8,9},{9,10},{10,1... | collective-permute-start | bytes 208904 | tf_op jit(solution)/shard_map/ppermute | solution.py:344
  37.7 5.0 %collective-permute-start.4 = (s32[2,1,8]{2,1,0:T(1,128)S(1)}, s32[2,1,8]{2,1,0:T(1,128)S(1)}, u32[]{:S(2)}, u32[]{:S(2)}) collective-permute-start(s32[2,1,8]{2,1,0:T(1,128)S(1)} %copy-done.5), channel_id=1, source_target_pairs={{0,1},{1,2},{2,3},{3,4},{4,5},{5,6},{6,7},{7,0},{8,9},{9,10},{10,1... | collective-permute-start | bytes 200 | tf_op jit(solution)/shard_map/ppermute | solution.py:344
  42.6 21.3 %collective-permute-start.6 = (f32[1024,384]{1,0:T(8,128)}, f32[1024,384]{1,0:T(8,128)S(1)}, u32[]{:S(2)}, u32[]{:S(2)}) collective-permute-start(f32[1024,384]{1,0:T(8,128)} %copy-done.2), channel_id=1, source_target_pairs={{0,1},{1,2},{2,3},{3,4},{4,5},{5,6},{6,7},{7,0},{8,9},{9,10},{10,1... | collective-permute-start | bytes 4718600 | tf_op jit(solution)/shard_map/ppermute | solution.py:344
  70.2 56.6 %collective-permute-start.11 = (f32[1024,640]{1,0:T(8,128)}, f32[1024,640]{1,0:T(8,128)}, u32[]{:S(2)}, u32[]{:S(2)}) collective-permute-start(f32[1024,640]{1,0:T(8,128)} %get-tuple-element.21.early_ref), channel_id=1, source_target_pairs={{0,1},{1,2},{2,3},{3,4},{4,5},{5,6},{6,7},{7,0},{8,9},{9,10},{10,1... | collective-permute-start | bytes 7864328 | tf_op jit(solution)/shard_map/ppermute | solution.py:344
  70.2 1.7 %copy-start = (f32[1024,640]{1,0:T(8,128)S(1)}, f32[1024,640]{1,0:T(8,128)}, u32[]{:S(2)}) copy-start(f32[1024,640]{1,0:T(8,128)} %get-tuple-element.21.early_ref) | copy-start | bytes 7864324
  83.6 4.4 %collective-permute-start.7 = (f32[136,128]{1,0:T(8,128)S(1)}, f32[136,128]{1,0:T(8,128)S(1)}, u32[]{:S(2)}, u32[]{:S(2)}) collective-permute-start(f32[136,128]{1,0:T(8,128)S(1)} %reduce_sum.19), channel_id=1, source_target_pairs={{0,32},{8,40},{16,48},{24,56},{32,0},{40,8},{48,16},{56,24},{64,96... | collective-permute-start | bytes 208904 | tf_op jit(solution)/shard_map/ppermute | solution.py:333
  88.0 5.8 %collective-permute-start.8 = (f32[136,128]{1,0:T(8,128)S(1)}, f32[136,128]{1,0:T(8,128)S(1)}, u32[]{:S(2)}, u32[]{:S(2)}) collective-permute-start(f32[136,128]{1,0:T(8,128)S(1)} %add.21), channel_id=1, source_target_pairs={{0,64},{8,72},{16,80},{24,88},{32,96},{40,104},{48,112},{56,120},{... | collective-permute-start | bytes 208904 | tf_op jit(solution)/shard_map/ppermute | solution.py:333
  93.8 6.9 %collective-permute-start.9 = (f32[136,128]{1,0:T(8,128)S(1)}, f32[136,128]{1,0:T(8,128)S(1)}, u32[]{:S(2)}, u32[]{:S(2)}) collective-permute-start(f32[136,128]{1,0:T(8,128)S(1)} %add.22), channel_id=1, source_target_pairs={{0,224},{8,232},{16,240},{24,248},{32,192},{40,200},{48,208},{56,2... | collective-permute-start | bytes 208904 | tf_op jit(solution)/shard_map/ppermute | solution.py:333
  100.8 5.0 %collective-permute-start.10 = (f32[136,128]{1,0:T(8,128)S(1)}, f32[136,128]{1,0:T(8,128)S(1)}, u32[]{:S(2)}, u32[]{:S(2)}) collective-permute-start(f32[136,128]{1,0:T(8,128)S(1)} %add.23), channel_id=1, source_target_pairs={{0,1},{1,2},{2,3},{3,4},{4,5},{5,6},{6,7},{7,0},{8,9},{9,10},{10,1... | collective-permute-start | bytes 208904 | tf_op jit(solution)/shard_map/ppermute | solution.py:344
  105.7 21.1 %collective-permute-start.12 = (f32[1024,384]{1,0:T(8,128)S(1)}, f32[1024,384]{1,0:T(8,128)S(1)}, u32[]{:S(2)}, u32[]{:S(2)}) collective-permute-start(f32[1024,384]{1,0:T(8,128)S(1)} %get-tuple-element.24.late_ref), channel_id=1, source_target_pairs={{0,1},{1,2},{2,3},{3,4},{4,5},{5,6},{6,7},{7,0},{8,9},{9,10},{10,1... | collective-permute-start | bytes 4718600 | tf_op jit(solution)/shard_map/ppermute | solution.py:344

commit v4 on v3

v4 whole, which is shorter than its diff:
```python
import functools

import jax
import jax.numpy as jnp
from jax import lax
from jax.experimental import pallas as pl
from jax.experimental.pallas import tpu as pltpu
from jax.sharding import PartitionSpec as P

WIDTH = 128
PAIRS = 4
PLACES = 2 * PAIRS
EARLY = 5
PANEL = 32
PACK = WIDTH // PANEL
SUB = 8
GROUP = 8
GROUP_ROWS = 136
HP = lax.Precision.HIGHEST
PARAMS = pltpu.CompilerParams(vmem_limit_bytes=28 * 1024 * 1024)


def split(value):
    high = value.astype(jnp.bfloat16)
    return high, (value - high.astype(jnp.float32)).astype(jnp.bfloat16)


def column_block(array, place):
    return array.at[:, pl.ds(place * WIDTH, WIDTH)]


def gram_pair(first, second, out_ref):
    a, b, c = split3(first)
    d, e, f = split3(second)
    large = contract(jnp.concatenate([a, b], axis=1), jnp.concatenate([d, e], axis=1), 0)
    small = contract(a, f, 0) + contract(c, d, 0)
    middle = large[:WIDTH, WIDTH:] + large[WIDTH:, :WIDTH]
    out_ref[:WIDTH, :] = large[:WIDTH, :WIDTH] + (middle + (large[WIDTH:, WIDTH:] + small))
    line = lax.broadcasted_iota(jnp.int32, (GROUP_ROWS - WIDTH, WIDTH), 0)
    norms = [jnp.sum(block * block, axis=0, keepdims=True) for block in (first, second)]
    out_ref[WIDTH:, :] = jnp.where(line == 0, norms[0], jnp.where(line == 1, norms[1], 0.0))


def first_gram_kernel(plan_ref, x_ref, gram_ref, early_ref, late_ref, held, sems, out_sems, plan, plan_sem):
    load_plan = pltpu.make_async_copy(plan_ref, plan, plan_sem)
    load_plan.start()
    loads = [
        pltpu.make_async_copy(column_block(x_ref, place), held.at[place], sems.at[place]) for place in range(PLACES)
    ]
    for copy in loads:
        copy.start()
    copies = []
    for place in range(PLACES):
        loads[place].wait()
        target = early_ref.at[place] if place < EARLY else late_ref.at[place - EARLY]
        copies.append(pltpu.make_async_copy(held.at[place], target, out_sems.at[place]))
        copies[-1].start()
    load_plan.wait()
    for pair in range(PAIRS):
        gram_pair(held[plan[0, 0, 2 * pair]], held[plan[0, 0, 2 * pair + 1]], gram_ref.at[pair])
    for copy in copies:
        copy.wait()


SUMS = jax.ShapeDtypeStruct((PAIRS, GROUP_ROWS, WIDTH), jnp.float32)


def blocks(count, height):
    return pltpu.HBM((count, height, WIDTH), jnp.float32)


def in_hbm(*arrays):
    return tuple(pltpu.with_memory_space_constraint(array, pltpu.HBM) for array in arrays)


def specs(*spaces):
    return [pl.BlockSpec(memory_space=space) for space in spaces]


def first_gram(x, plan):
    height = x.shape[0]
    return pl.pallas_call(
        first_gram_kernel,
        out_shape=(SUMS, blocks(EARLY, height), blocks(PLACES - EARLY, height)),
        in_specs=specs(pltpu.HBM, pltpu.HBM),
        out_specs=specs(pltpu.VMEM, pltpu.HBM, pltpu.HBM),
        scratch_shapes=[
            pltpu.VMEM((PLACES, height, WIDTH), jnp.float32),
            pltpu.SemaphoreType.DMA((PLACES,)),
            pltpu.SemaphoreType.DMA((PLACES,)),
            pltpu.SMEM(plan.shape, jnp.int32),
            pltpu.SemaphoreType.DMA,
        ],
        compiler_params=PARAMS,
        name="first_gram",
    )(*in_hbm(plan, x))


def panel_inverse(block):
    parts = [block[i : i + SUB, :] for i in range(0, PANEL, SUB)]
    row = lax.broadcasted_iota(jnp.int32, (SUB, WIDTH), 0)
    lane = lax.broadcasted_iota(jnp.int32, (SUB, WIDTH), 1)
    base = (lane // PANEL) * PANEL
    inner = lane - base

    def line(value, j):
        return jnp.broadcast_to(value[j // SUB][j % SUB : j % SUB + 1, :], (SUB, WIDTH))

    def column(value, j):
        return [jnp.take_along_axis(part, base + j, axis=1) for part in value]

    for start in range(0, PANEL, GROUP):
        columns = [column(parts, j) for j in range(start, start + GROUP)]
        for j in range(start, start + GROUP, 2):
            c0, c1, *columns = columns
            a, b, d = line(c0, j), line(c1, j), line(c1, j + 1)
            r = 1.0 / (a * d - b * b)

            def update(value, u, v, cleared):
                m0, m1 = (d * u - b * v), (a * v - b * u)
                out = []
                for i in range(len(value)):
                    old = value[i] if cleared is None else jnp.where(cleared, 0.0, value[i])
                    out.append(old - (c0[i] * m0 + c1[i] * m1) * r)
                i = j // SUB
                out[i] = jnp.where(row == j % SUB, m0 * r, jnp.where(row == j % SUB + 1, m1 * r, out[i]))
                return out
            columns = [update(c, line(c, j), line(c, j + 1), None) for c in columns]
            at0, at1 = inner == j, inner == j + 1
            u = jnp.where(at0, 1.0, jnp.where(at1, 0.0, line(parts, j)))
            v = jnp.where(at1, 1.0, jnp.where(at0, 0.0, line(parts, j + 1)))
            parts = update(parts, u, v, at0 | at1)
    return jnp.concatenate(parts, axis=0)


def split3(value):
    high = value.astype(jnp.bfloat16)
    rest = value - high.astype(jnp.float32)
    middle = rest.astype(jnp.bfloat16)
    return high, middle, (rest - middle.astype(jnp.float32)).astype(jnp.bfloat16)


def contract(left, right, over):
    return lax.dot_general(left, right, (((over,), (over,)), ((), ())), preferred_element_type=jnp.float32)


def tall_dot(left, right):
    (a, b, c), (d, e, f) = left, right
    return contract(jnp.concatenate([a, b, a, b, c, a], axis=0), jnp.concatenate([d, d, e, e, d, f], axis=0), 0)


def square_dot(left, right, over):
    (a, b, c), (d, e, f) = left, right
    pair = lambda x, y: jnp.concatenate([x, y], axis=over)
    return contract(pair(a, b), pair(d, e), over) + (
        contract(pair(a, b), pair(e, d), over) + contract(pair(a, c), pair(f, d), over)
    )


def rotations(sums, count):
    width = WIDTH
    row = lax.broadcasted_iota(jnp.int32, (width, width), 0)
    lane = lax.broadcasted_iota(jnp.int32, (width, width), 1)
    eye = (row == lane).astype(jnp.float32)
    halves, systems = [], []
    for pair in range(count):
        cross = sums[pair][:width, :]
        scale = lax.rsqrt(sums[pair][width:, :] + 1e-06)
        down = jnp.sum(eye * scale[0:1, :], axis=1, keepdims=True)
        half = 0.5 * cross * down * scale[1:2, :]
        parts = split3(half)
        spd = eye + square_dot(parts, parts, 1)
        halves.append((half, parts))
        systems.append(jnp.concatenate([spd, half], axis=1))
    group = lax.broadcasted_iota(jnp.int32, (PANEL, width), 1) // PANEL
    wide = lax.broadcasted_iota(jnp.int32, (PANEL, 2 * width), 1)
    wide_row = lax.broadcasted_iota(jnp.int32, (PANEL, 2 * width), 0)
    for panel in range(width // PANEL):
        lo, hi = panel * PANEL, (panel + 1) * PANEL
        inside = (wide >= lo) & (wide < hi)
        cleared = jnp.concatenate([inside] * (width // PANEL), axis=0)
        done = []
        for first in range(0, count, PACK):
            members = range(first, min(first + PACK, count))
            packed = None
            for pair in members:
                part = systems[pair][lo:hi, :width]
                shift = ((pair - first) * PANEL - lo) % width
                if shift:
                    part = pltpu.roll(part, shift, 1)
                packed = part if packed is None else jnp.where(group == pair - first, part, packed)
            inverse = split3(panel_inverse(packed))
            for pair in members:
                old = systems[pair]
                top = old[lo:hi, :]
                unit = jnp.where(inside, (wide - lo == wide_row).astype(jnp.float32), top)
                at = (pair - first) * PANEL
                fresh = tall_dot(inverse, split3(unit))[at : at + PANEL, :]
                side = jnp.where(lane[:PANEL] < lo, -top[:, :width], top[:, :width])
                change = tall_dot(split3(side), split3(fresh))
                updated = jnp.where(cleared, 0.0, old) - change
                done.append(jnp.concatenate(([updated[:lo]] if lo else []) + [fresh] + ([updated[hi:]] if hi < width else []), axis=0))
        systems = done
    return [(halves[pair][0], systems[pair][:, :width], systems[pair][:, width:]) for pair in range(count)]


def write_sides(sums_ref, sides_ref):
    width = WIDTH
    row = lax.broadcasted_iota(jnp.int32, (width, width), 0)
    lane = lax.broadcasted_iota(jnp.int32, (width, width), 1)
    eye = (row == lane).astype(jnp.float32)
    sums = [sums_ref.at[pair, which] for which in range(2) for pair in range(PAIRS)]

    def write(index, top, bottom):
        for start, part in ((0, top), (width, bottom)):
            high, low = split(part)
            sides_ref[index, start : start + width, :width] = high
            sides_ref[index, start : start + width, width:] = low

    for index, (half, inverse, across) in enumerate(rotations(sums, len(sums))):
        if index >= PAIRS:
            write(index, 2.0 * across, eye - 2.0 * square_dot(split3(half), split3(across), 0))
        left = index if index < PAIRS else index + PAIRS
        if left < sides_ref.shape[0]:
            write(left, 2.0 * inverse - eye, -2.0 * across.T)


def rotate_kernel(sums_ref, early_ref, late_ref, sides_ref, own_ref, sems):
    start_loads(sent_blocks(early_ref, late_ref), own_ref, sems)
    write_sides(sums_ref, sides_ref)
    wait_loads(own_ref, sems, range(PLACES))


def rotate(sums, own):
    return pl.pallas_call(
        rotate_kernel,
        out_shape=(
            jax.ShapeDtypeStruct((3 * PAIRS, 2 * WIDTH, 2 * WIDTH), jnp.bfloat16),
            pltpu.VMEM((PLACES, own[0].shape[1], WIDTH), jnp.float32),
        ),
        in_specs=specs(pltpu.VMEM, pltpu.HBM, pltpu.HBM),
        out_specs=specs(pltpu.VMEM, pltpu.VMEM),
        scratch_shapes=[pltpu.SemaphoreType.DMA((PLACES,))],
        compiler_params=PARAMS,
        name="rotate",
    )(sums, *in_hbm(*own))


def turned_pair(held, both, side):
    high, low = split(jnp.concatenate([held[place] for place in both], axis=1))
    parts = jnp.dot(high, side, preferred_element_type=jnp.float32)
    rest = jnp.dot(low, side[:, :WIDTH], preferred_element_type=jnp.float32)
    return parts[:, :WIDTH] + (parts[:, WIDTH:] + rest)


def start_loads(sources, held, sems):
    for place, source in enumerate(sources):
        pltpu.make_async_copy(source, held.at[place], sems.at[place]).start()


def wait_loads(held, sems, both):
    for place in both:
        pltpu.make_async_copy(held.at[0], held.at[place], sems.at[place]).wait()


def load_plans(refs, plan, sems):
    copies = [pltpu.make_async_copy(ref, plan.at[which], sems.at[which]) for which, ref in enumerate(refs)]
    for copy in copies:
        copy.start()
    return copies


def sent_blocks(early_ref, late_ref):
    return [early_ref.at[place] if place < EARLY else late_ref.at[place - EARLY] for place in range(PLACES)]


def both_of(plan, which, step, pair):
    return [plan[which, step, 0, 2 * pair + i] for i in range(2)]


def turn_all(step, own, prev, prev_sems, sides_ref, turned, outs, out_sems, plan):
    copies = []
    for which, held in enumerate((own, prev)):
        for pair in range(PAIRS):
            both = both_of(plan, which, step, pair)
            if which:
                wait_loads(prev, prev_sems, both)
            place = 2 * pair + which
            turned[place] = turned_pair(held, both, sides_ref[which * PAIRS + pair])
            target = column_block(outs[0], place) if len(outs) == 1 else outs[which].at[pair]
            copies.append(pltpu.make_async_copy(turned.at[place], target, out_sems.at[place]))
            copies[-1].start()
    return copies


def first_turn_kernel(
    sides_ref, own_ref, early_ref, late_ref, own_plan_ref, prev_plan_ref,
    gram_ref, stay_ref, moved_ref, held, turned, in_sems, out_sems, plan, plan_sems,
):
    plans = load_plans((own_plan_ref, prev_plan_ref), plan, plan_sems)
    start_loads(sent_blocks(early_ref, late_ref), held, in_sems)
    for copy in plans:
        copy.wait()
    copies = turn_all(0, own_ref, held, in_sems, sides_ref, turned, (stay_ref, moved_ref), out_sems, plan)
    for pair in range(PAIRS):
        first, second = [turned[place] for place in both_of(plan, 0, 1, pair)]
        gram_pair(first, second, gram_ref.at[pair])
    for copy in copies:
        copy.wait()


def first_turn(sides, own, prev, plans):
    height = own.shape[1]
    return pl.pallas_call(
        first_turn_kernel,
        out_shape=(SUMS, blocks(PAIRS, height), blocks(PAIRS, height)),
        in_specs=specs(pltpu.VMEM, pltpu.VMEM, *[pl.ANY] * 4),
        out_specs=specs(pltpu.VMEM, pltpu.HBM, pltpu.HBM),
        scratch_shapes=[
            pltpu.VMEM((PLACES, height, WIDTH), jnp.float32),
            pltpu.VMEM((PLACES, height, WIDTH), jnp.float32),
            pltpu.SemaphoreType.DMA((PLACES,)),
            pltpu.SemaphoreType.DMA((PLACES,)),
            pltpu.SMEM((2,) + plans[0].shape, jnp.int32),
            pltpu.SemaphoreType.DMA((2,)),
        ],
        compiler_params=PARAMS,
        name="first_turn",
    )(sides, own, *prev, *plans)


def prev_stay_kernel(sides_ref, early_ref, late_ref, plan_ref, out_ref, turned, out_sems, held, in_sems, plan, plan_sem):
    load_plan = pltpu.make_async_copy(plan_ref, plan.at[0], plan_sem)
    load_plan.start()
    start_loads(sent_blocks(early_ref, late_ref), held, in_sems)
    load_plan.wait()
    copies = []
    for pair in range(PAIRS):
        both = both_of(plan, 0, 0, pair)
        wait_loads(held, in_sems, both)
        turned[pair] = turned_pair(held, both, sides_ref[2 * PAIRS + pair])
        copies.append(pltpu.make_async_copy(turned.at[pair], out_ref.at[pair], out_sems.at[pair]))
        copies[-1].start()
    for copy in copies:
        copy.wait()


def prev_stay(sides, prev, plan):
    height = prev[0].shape[1]
    return pl.pallas_call(
        prev_stay_kernel,
        out_shape=blocks(PAIRS, height),
        in_specs=specs(pltpu.VMEM, *[pl.ANY] * 3),
        out_specs=pl.BlockSpec(memory_space=pltpu.HBM),
        scratch_shapes=[
            pltpu.VMEM((PAIRS, height, WIDTH), jnp.float32),
            pltpu.SemaphoreType.DMA((PAIRS,)),
            pltpu.VMEM((PLACES, height, WIDTH), jnp.float32),
            pltpu.SemaphoreType.DMA((PLACES,)),
            pltpu.SMEM((1,) + plan.shape, jnp.int32),
            pltpu.SemaphoreType.DMA,
        ],
        compiler_params=PARAMS,
        name="prev_stay",
    )(sides, *prev, plan)


def last_turn_kernel(
    sums_ref, own_stay_ref, own_moved_ref, stay_ref, moved_ref, own_plan_ref, prev_plan_ref,
    out_ref, sides, held, turned, in_sems, out_sems, plan, plan_sems,
):
    plans = load_plans((own_plan_ref, prev_plan_ref), plan, plan_sems)
    for which, refs in enumerate(((own_stay_ref, own_moved_ref), (stay_ref, moved_ref))):
        start_loads([refs[place % 2].at[place // 2] for place in range(PLACES)], held.at[which], in_sems.at[which])
    write_sides(sums_ref, sides)
    for copy in plans:
        copy.wait()
    wait_loads(held.at[0], in_sems.at[0], range(PLACES))
    for copy in turn_all(1, held.at[0], held.at[1], in_sems.at[1], sides, turned, (out_ref,), out_sems, plan):
        copy.wait()


def last_turn(sums, own, prev_stayed, prev_moved, plans):
    height = own[0].shape[1]
    return pl.pallas_call(
        last_turn_kernel,
        out_shape=jax.ShapeDtypeStruct((height, PLACES * WIDTH), jnp.float32),
        in_specs=specs(pltpu.VMEM, *[pltpu.HBM] * 3, *[pl.ANY] * 3),
        out_specs=pl.BlockSpec(memory_space=pltpu.HBM),
        scratch_shapes=[
            pltpu.VMEM((2 * PAIRS, 2 * WIDTH, 2 * WIDTH), jnp.bfloat16),
            pltpu.VMEM((2, PLACES, height, WIDTH), jnp.float32),
            pltpu.VMEM((PLACES, height, WIDTH), jnp.float32),
            pltpu.SemaphoreType.DMA((2, PLACES)),
            pltpu.SemaphoreType.DMA((PLACES,)),
            pltpu.SMEM((2,) + plans[0].shape, jnp.int32),
            pltpu.SemaphoreType.DMA((2,)),
        ],
        compiler_params=PARAMS,
        name="last_turn",
    )(sums, *in_hbm(*own, prev_stayed), prev_moved, *plans)


def onward(value):
    count = lax.axis_size("pairs")
    return lax.ppermute(value, "pairs", [(q, (q + 1) % count) for q in range(count)])


def row_groups():
    return [list(range(start, start + PAIRS)) for start in range(0, lax.axis_size("rows"), PAIRS)]


def summed_mine(parts):
    count = lax.axis_size("rows")
    nx, nz = PAIRS, count // PAIRS
    mine = jnp.sum(lax.all_to_all(parts, "rows", 0, 0, axis_index_groups=row_groups()), axis=0)
    step = 1
    while step < nz:
        turned = nz - 1 if 2 * step == nz else step
        mine = mine + lax.ppermute(mine, "rows", [(i, (((i // nx) ^ turned) * nx) + i % nx) for i in range(count)])
        step *= 2
    return mine


def gathered(mine, theirs):
    both = jnp.stack([mine, theirs])
    return lax.all_to_all(jnp.broadcast_to(both, (PAIRS,) + both.shape), "rows", 0, 0, axis_index_groups=row_groups())


def local(snapshot, plan):
    parts, early, late = first_gram(snapshot, plan)
    prev_early = onward(early)
    mine = summed_mine(parts)
    theirs, prev_plan, sent = lax.optimization_barrier((onward(mine), onward(plan), late))
    prev = (prev_early, onward(sent))
    plans = (plan, prev_plan)
    sides, own = rotate(gathered(mine, theirs), (early, late))
    parts, stay, moved = first_turn(sides, own, prev, plans)
    prev_moved = onward(moved)
    mine = summed_mine(parts)
    theirs = onward(mine)
    prev_stayed = prev_stay(sides, lax.optimization_barrier((prev, mine))[0], prev_plan)
    return last_turn(gathered(mine, theirs), (stay, moved), prev_stayed, prev_moved, plans)


def solution(mesh):
    return jax.shard_map(
        local,
        mesh=mesh,
        in_specs=(P("rows", "pairs"), P(None, "pairs", None)),
        out_specs=P("rows", "pairs"),
        check_vma=False,
    )
```

time: 133 us -> 124 us (0.932)
  blocking collectives: 45.2 us -> 33 us
  starting transfers between devices: 17.1 us -> 24.2 us
  waiting for transfers between devices: 34 us -> 30.6 us
    all_to_all x4 -> x3, blocking collectives: 45.2 us -> 33 us  [the longest x2 20.1 us: summed_mine(): lax.all_to_all(parts, 'rows', 0, 0, axis_index_groups=row_groups())]
    all_to_all x0 -> x1, starting transfers between devices: none -> 4.9 us  [gathered(): lax.all_to_all(jnp.broadcast_to(both, (PAIRS,) + both.shape), 'rows', 0,...]
    ppermute x7 -> x6, waiting for transfers between devices: 13.1 us -> 10.1 us  [onward(): lax.ppermute(value, 'pairs', [(q, (q + 1) % count) for q in range(count)])]
    ppermute x6, starting transfers between devices: 16.1 us -> 17.8 us  [summed_mine(): lax.ppermute(mine, 'rows', [(i, (i // nx ^ turned) * nx + i % nx) for i i...]
    pallas_call x6 -> x5, Pallas kernels: 32.5 us -> 31.4 us  [the longest x1 11.2 us: last_turn(): pl.pallas_call(last_turn_kernel, out_shape=jax.ShapeDtypeStruct((height,...]
    unnamed x12 -> x10, local copies, waits for them, and re-layouts: 3.58 us -> 2.83 us
  transfers between devices with their start and end apart: 13 -> 13, of which waited for: 10 -> 10; matrix products, arithmetic and copies ran while one was open for 0% -> 1% of each run, Pallas kernels for 12% -> 8%
where the time goes in v4:
time: 124 us; the launch traced here: 123 us
  blocking collectives  33 us (27%)
  Pallas kernels  31.4 us (25%)
  waiting for transfers between devices  30.6 us (25%)
  starting transfers between devices  24.2 us (20%)
  local copies, waits for them, and re-layouts  3.7 us (3%)
    all_to_all x2, blocking collectives, summed_mine(): lax.all_to_all(parts, 'rows', 0, 0, axis_index_groups=row_groups())  20.1 us
    ppermute x6, waiting for transfers between devices, summed_mine(): lax.ppermute(mine, 'rows', [(i, (i // nx ^ turned) * nx + i % nx) for i i...  19.7 us
    ppermute x6, starting transfers between devices, summed_mine(): lax.ppermute(mine, 'rows', [(i, (i // nx ^ turned) * nx + i % nx) for i i...  17.8 us
    all_to_all x1, blocking collectives, gathered(): lax.all_to_all(jnp.broadcast_to(both, (PAIRS,) + both.shape), 'rows', 0,...  12.9 us
    pallas_call x1, Pallas kernels, last_turn(): pl.pallas_call(last_turn_kernel, out_shape=jax.ShapeDtypeStruct((height,...  11.2 us
    ppermute x6, waiting for transfers between devices, onward(): lax.ppermute(value, 'pairs', [(q, (q + 1) % count) for q in range(count)])  10.1 us
    pallas_call x1, Pallas kernels, rotate(): pl.pallas_call(rotate_kernel, out_shape=(jax.ShapeDtypeStruct((3 * PAIRS,...  6.6 us
    pallas_call x1, Pallas kernels, first_turn(): pl.pallas_call(first_turn_kernel, out_shape=(SUMS, blocks(PAIRS, height),...  5.6 us
  transfers between devices with their start and end apart: 13, of which 10 were waited for; matrix products, arithmetic and copies ran while one was open for 1% of the time, Pallas kernels for 8%

profile of v4, /device:TPU:2, one launch (start us, length us, event | category | flops | bytes accessed | tf_op | source)
XLA Modules:
  0.0 123.3 jit_solution(11464304172579576847)
XLA Ops:
  0.0 4.7 %first_gram.1 = (f32[4,136,128]{2,1,0:T(8,128)S(1)}, f32[5,1024,128]{2,1,0:T(8,128)}, f32[3,1024,128]{2,1,0:T(8,128)}) custom-call(s32[2,1,8]{2,1,0:T(1,128)} %own_plan_ref.3, f32[1024,1024]{1,0:T(8,128)} %x_ref.1), custom_call_target="tpu_custom_call" | custom-call | tf_op jit(solution)/shard_map/first_gram/pallas_call | solution.py:82
  4.8 11.1 %all_to_all.20 = f32[4,136,128]{2,1,0:T(8,128)S(1)} all-to-all(f32[4,136,128]{2,1,0:T(8,128)S(1)} %get-tuple-element.18), channel_id=1, replica_groups={{0,8,16,24},{32,40,48,56},{64,72,80,88},{96,104,112,120},{128,136,144,1..., dimensions={0} | all-to-all | bytes 557056 | tf_op jit(solution)/shard_map/all_to_all | solution.py:416
  15.9 2.0 %collective-permute-start = (f32[136,128]{1,0:T(8,128)S(1)}, f32[136,128]{1,0:T(8,128)S(1)}, u32[]{:S(2)}, u32[]{:S(2)}) collective-permute-start(f32[136,128]{1,0:T(8,128)S(1)} %reduce_sum.18), channel_id=1, source_target_pairs={{0,32},{8,40},{16,48},{24,56},{32,0},{40,8},{48,16},{56,24},{64,96... | collective-permute-start | bytes 208904 | tf_op jit(solution)/shard_map/ppermute | solution.py:420
  17.9 2.8 %collective-permute-done = f32[136,128]{1,0:T(8,128)S(1)} collective-permute-done((f32[136,128]{1,0:T(8,128)S(1)}, f32[136,128]{1,0:T(8,128)S(1)}, u32[]{:S(2)}, u32[]{:S(2)}) %collective-permute-start) | collective-permute-done | bytes 69664 | tf_op jit(solution)/shard_map/ppermute | solution.py:420
  20.7 3.4 %collective-permute-start.1 = (f32[136,128]{1,0:T(8,128)S(1)}, f32[136,128]{1,0:T(8,128)S(1)}, u32[]{:S(2)}, u32[]{:S(2)}) collective-permute-start(f32[136,128]{1,0:T(8,128)S(1)} %add.18), channel_id=1, source_target_pairs={{0,64},{8,72},{16,80},{24,88},{32,96},{40,104},{48,112},{56,120},{... | collective-permute-start | bytes 208904 | tf_op jit(solution)/shard_map/ppermute | solution.py:420
  24.1 3.8 %collective-permute-done.1 = f32[136,128]{1,0:T(8,128)S(1)} collective-permute-done((f32[136,128]{1,0:T(8,128)S(1)}, f32[136,128]{1,0:T(8,128)S(1)}, u32[]{:S(2)}, u32[]{:S(2)}) %collective-permute-start.1) | collective-permute-done | bytes 69664 | tf_op jit(solution)/shard_map/ppermute | solution.py:420
  27.8 4.9 %collective-permute-start.2 = (f32[136,128]{1,0:T(8,128)S(1)}, f32[136,128]{1,0:T(8,128)S(1)}, u32[]{:S(2)}, u32[]{:S(2)}) collective-permute-start(f32[136,128]{1,0:T(8,128)S(1)} %add.19), channel_id=1, source_target_pairs={{0,224},{8,232},{16,240},{24,248},{32,192},{40,200},{48,208},{56,2... | collective-permute-start | bytes 208904 | tf_op jit(solution)/shard_map/ppermute | solution.py:420
  32.7 2.6 %collective-permute-done.2 = f32[136,128]{1,0:T(8,128)S(1)} collective-permute-done((f32[136,128]{1,0:T(8,128)S(1)}, f32[136,128]{1,0:T(8,128)S(1)}, u32[]{:S(2)}, u32[]{:S(2)}) %collective-permute-start.2) | collective-permute-done | bytes 69664 | tf_op jit(solution)/shard_map/ppermute | solution.py:420
  35.4 1.4 %collective-permute-start.4 = (s32[2,1,8]{2,1,0:T(1,128)S(1)}, s32[2,1,8]{2,1,0:T(1,128)S(1)}, u32[]{:S(2)}, u32[]{:S(2)}) collective-permute-start(s32[2,1,8]{2,1,0:T(1,128)S(1)} %copy-done.4), channel_id=1, source_target_pairs={{0,1},{1,2},{2,3},{3,4},{4,5},{5,6},{6,7},{7,0},{8,9},{9,10},{10,1... | collective-permute-start | bytes 200 | tf_op jit(solution)/shard_map/ppermute | solution.py:406
  36.8 3.5 %collective-permute-done.4.prev_plan_ref.plan_ref = s32[2,1,8]{2,1,0:T(1,128)S(1)} collective-permute-done((s32[2,1,8]{2,1,0:T(1,128)S(1)}, s32[2,1,8]{2,1,0:T(1,128)S(1)}, u32[]{:S(2)}, u32[]{:S(2)}) %collective-permute-start.4) | collective-permute-done | bytes 96 | tf_op jit(solution)/shard_map/ppermute | solution.py:406
  40.4 12.9 %all_to_all.21.sums_ref = f32[4,2,136,128]{3,2,1,0:T(8,128)S(1)} all-to-all(f32[4,2,136,128]{3,2,1,0:T(8,128)S(1)} %broadcast_in_dim.6), channel_id=1, replica_groups={{0,8,16,24},{32,40,48,56},{64,72,80,88},{96,104,112,120},{128,136,144,1..., dimensions={0} | all-to-all | bytes 1114112 | tf_op jit(solution)/shard_map/all_to_all | solution.py:427
  53.3 6.6 %rotate.1 = (bf16[12,256,256]{2,1,0:T(8,128)(2,1)S(1)}, f32[8,1024,128]{2,1,0:T(8,128)S(1)}) custom-call(f32[4,2,136,128]{3,2,1,0:T(8,128)S(1)} %all_to_all.21.sums_ref, f32[5,1024,128]{2,1,0:T(8,128)} %get-tuple-element.21.early_ref, f32[3,1024,128]{2,1,0:T(8,128)} %get-tuple-element.24.late_ref), custom_call_target="tpu_custom_call" | custom-call | tf_op jit(solution)/shard_map/rotate/pallas_call | solution.py:235
  60.0 1.7 %collective-permute-done.6.late_ref = f32[3,1024,128]{2,1,0:T(8,128)S(1)} collective-permute-done((f32[3,1024,128]{2,1,0:T(8,128)}, f32[3,1024,128]{2,1,0:T(8,128)S(1)}, u32[]{:S(2)}, u32[]{:S(2)}) %collective-permute-start.6) | collective-permute-done | bytes 1572896 | tf_op jit(solution)/shard_map/ppermute | solution.py:406
  61.6 5.6 %first_turn.1 = (f32[4,136,128]{2,1,0:T(8,128)S(1)}, f32[4,1024,128]{2,1,0:T(8,128)}, f32[4,1024,128]{2,1,0:T(8,128)}) custom-call(bf16[12,256,256]{2,1,0:T(8,128)(2,1)S(1)} %get-tuple-element.22.sides_ref, f32[8,1024,128]{2,1,0:T(8,128)S(1)} %get-tuple-element.23.own_ref, f32[5,1024,128]{2,1,0:T(8,128)S(1)} %collective-permute-done.5.early_ref, ...), custom_call_target="tpu_custom_call" | custom-call | tf_op jit(solution)/shard_map/first_turn/pallas_call | solution.py:314
  67.3 9.0 %all_to_all.22 = f32[4,136,128]{2,1,0:T(8,128)S(1)} all-to-all(f32[4,136,128]{2,1,0:T(8,128)S(1)} %get-tuple-element.26), channel_id=1, replica_groups={{0,8,16,24},{32,40,48,56},{64,72,80,88},{96,104,112,120},{128,136,144,1..., dimensions={0} | all-to-all | bytes 557056 | tf_op jit(solution)/shard_map/all_to_all | solution.py:416
  77.1 3.6 %collective-permute-done.7 = f32[136,128]{1,0:T(8,128)S(1)} collective-permute-done((f32[136,128]{1,0:T(8,128)S(1)}, f32[136,128]{1,0:T(8,128)S(1)}, u32[]{:S(2)}, u32[]{:S(2)}) %collective-permute-start.7) | collective-permute-done | bytes 69664 | tf_op jit(solution)/shard_map/ppermute | solution.py:420
  80.7 2.2 %collective-permute-start.8 = (f32[136,128]{1,0:T(8,128)S(1)}, f32[136,128]{1,0:T(8,128)S(1)}, u32[]{:S(2)}, u32[]{:S(2)}) collective-permute-start(f32[136,128]{1,0:T(8,128)S(1)} %add.21), channel_id=1, source_target_pairs={{0,64},{8,72},{16,80},{24,88},{32,96},{40,104},{48,112},{56,120},{... | collective-permute-start | bytes 208904 | tf_op jit(solution)/shard_map/ppermute | solution.py:420
  82.9 4.0 %collective-permute-done.8 = f32[136,128]{1,0:T(8,128)S(1)} collective-permute-done((f32[136,128]{1,0:T(8,128)S(1)}, f32[136,128]{1,0:T(8,128)S(1)}, u32[]{:S(2)}, u32[]{:S(2)}) %collective-permute-start.8) | collective-permute-done | bytes 69664 | tf_op jit(solution)/shard_map/ppermute | solution.py:420
  87.0 4.6 %collective-permute-start.9 = (f32[136,128]{1,0:T(8,128)S(1)}, f32[136,128]{1,0:T(8,128)S(1)}, u32[]{:S(2)}, u32[]{:S(2)}) collective-permute-start(f32[136,128]{1,0:T(8,128)S(1)} %add.22), channel_id=1, source_target_pairs={{0,224},{8,232},{16,240},{24,248},{32,192},{40,200},{48,208},{56,2... | collective-permute-start | bytes 208904 | tf_op jit(solution)/shard_map/ppermute | solution.py:420
  91.6 2.8 %collective-permute-done.9 = f32[136,128]{1,0:T(8,128)S(1)} collective-permute-done((f32[136,128]{1,0:T(8,128)S(1)}, f32[136,128]{1,0:T(8,128)S(1)}, u32[]{:S(2)}, u32[]{:S(2)}) %collective-permute-start.9) | collective-permute-done | bytes 69664 | tf_op jit(solution)/shard_map/ppermute | solution.py:420
  94.4 4.9 %collective-permute-done.10 = f32[136,128]{1,0:T(8,128)S(1)} collective-permute-done((f32[136,128]{1,0:T(8,128)S(1)}, f32[136,128]{1,0:T(8,128)S(1)}, u32[]{:S(2)}, u32[]{:S(2)}) %collective-permute-start.10) | collective-permute-done | bytes 69664 | tf_op jit(solution)/shard_map/ppermute | solution.py:406
  100.2 4.9 %all-to-all-start.3 = ((f32[4,2,136,128]{3,2,1,0:T(8,128)}), f32[4,2,136,128]{3,2,1,0:T(8,128)S(1)}, u32[]{:S(2)}, u32[]{:S(2)}) async-start(f32[4,2,136,128]{3,2,1,0:T(8,128)} %broadcast_in_dim.7), calls=%async_computation.3 | async-start | bytes 1114112 | tf_op jit(solution)/shard_map/all_to_all | solution.py:427
  107.9 3.3 %prev_stay.1.stay_ref = f32[4,1024,128]{2,1,0:T(8,128)} custom-call(bf16[12,256,256]{2,1,0:T(8,128)(2,1)S(1)} %copy-done.3, f32[5,1024,128]{2,1,0:T(8,128)S(1)} %collective-permute-done.5.early_ref, f32[3,1024,128]{2,1,0:T(8,128)S(1)} %copy-done.1, s32[2,1,8]{2,1,0:T(1,128)S(1)} %collective-permute-done.4.prev_plan_ref.plan_ref), custom_call_target="tpu_custom_call" | custom-call | tf_op jit(solution)/shard_map/prev_stay/pallas_call | solution.py:350
  111.9 11.2 %last_turn.1 = f32[1024,1024]{1,0:T(8,128)} custom-call(f32[4,2,136,128]{3,2,1,0:T(8,128)S(1)} %all-to-all-done.3.sums_ref, f32[4,1024,128]{2,1,0:T(8,128)} %get-tuple-element.27.own_stay_ref, f32[4,1024,128]{2,1,0:T(8,128)} %get-tuple-element.28.own_moved_ref, f32[4,1024,128]{2,1,0:T(8,128)} %prev_stay.1.stay_ref, ...), custom_call_target="tpu_custom_call" | custom-call | tf_op jit(solution)/shard_map/last_turn/pallas_call | solution.py:385
  (32 shorter events, 5.4 us)
Async XLA Ops:
  0.0 35.4 %copy-start.4 = (s32[2,1,8]{2,1,0:T(1,128)S(1)}, s32[2,1,8]{2,1,0:T(1,128)}, u32[]{:S(2)}) copy-start(s32[2,1,8]{2,1,0:T(1,128)} %own_plan_ref.3) | copy-start | bytes 196
  4.7 56.9 %collective-permute-start.5 = (f32[5,1024,128]{2,1,0:T(8,128)}, f32[5,1024,128]{2,1,0:T(8,128)S(1)}, u32[]{:S(2)}, u32[]{:S(2)}) collective-permute-start(f32[5,1024,128]{2,1,0:T(8,128)} %get-tuple-element.21.early_ref), channel_id=1, source_target_pairs={{0,1},{1,2},{2,3},{3,4},{4,5},{5,6},{6,7},{7,0},{8,9},{9,10},{10,1... | collective-permute-start | bytes 7864328 | tf_op jit(solution)/shard_map/ppermute | solution.py:406
  15.9 4.8 %collective-permute-start = (f32[136,128]{1,0:T(8,128)S(1)}, f32[136,128]{1,0:T(8,128)S(1)}, u32[]{:S(2)}, u32[]{:S(2)}) collective-permute-start(f32[136,128]{1,0:T(8,128)S(1)} %reduce_sum.18), channel_id=1, source_target_pairs={{0,32},{8,40},{16,48},{24,56},{32,0},{40,8},{48,16},{56,24},{64,96... | collective-permute-start | bytes 208904 | tf_op jit(solution)/shard_map/ppermute | solution.py:420
  20.7 7.1 %collective-permute-start.1 = (f32[136,128]{1,0:T(8,128)S(1)}, f32[136,128]{1,0:T(8,128)S(1)}, u32[]{:S(2)}, u32[]{:S(2)}) collective-permute-start(f32[136,128]{1,0:T(8,128)S(1)} %add.18), channel_id=1, source_target_pairs={{0,64},{8,72},{16,80},{24,88},{32,96},{40,104},{48,112},{56,120},{... | collective-permute-start | bytes 208904 | tf_op jit(solution)/shard_map/ppermute | solution.py:420
  27.8 7.5 %collective-permute-start.2 = (f32[136,128]{1,0:T(8,128)S(1)}, f32[136,128]{1,0:T(8,128)S(1)}, u32[]{:S(2)}, u32[]{:S(2)}) collective-permute-start(f32[136,128]{1,0:T(8,128)S(1)} %add.19), channel_id=1, source_target_pairs={{0,224},{8,232},{16,240},{24,248},{32,192},{40,200},{48,208},{56,2... | collective-permute-start | bytes 208904 | tf_op jit(solution)/shard_map/ppermute | solution.py:420
  35.4 5.0 %collective-permute-start.3 = (f32[136,128]{1,0:T(8,128)S(1)}, f32[136,128]{1,0:T(8,128)S(1)}, u32[]{:S(2)}, u32[]{:S(2)}) collective-permute-start(f32[136,128]{1,0:T(8,128)S(1)} %add.20), channel_id=1, source_target_pairs={{0,1},{1,2},{2,3},{3,4},{4,5},{5,6},{6,7},{7,0},{8,9},{9,10},{10,1... | collective-permute-start | bytes 208904 | tf_op jit(solution)/shard_map/ppermute | solution.py:406
  35.4 5.0 %collective-permute-start.4 = (s32[2,1,8]{2,1,0:T(1,128)S(1)}, s32[2,1,8]{2,1,0:T(1,128)S(1)}, u32[]{:S(2)}, u32[]{:S(2)}) collective-permute-start(s32[2,1,8]{2,1,0:T(1,128)S(1)} %copy-done.4), channel_id=1, source_target_pairs={{0,1},{1,2},{2,3},{3,4},{4,5},{5,6},{6,7},{7,0},{8,9},{9,10},{10,1... | collective-permute-start | bytes 200 | tf_op jit(solution)/shard_map/ppermute | solution.py:406
  40.4 21.3 %collective-permute-start.6 = (f32[3,1024,128]{2,1,0:T(8,128)}, f32[3,1024,128]{2,1,0:T(8,128)S(1)}, u32[]{:S(2)}, u32[]{:S(2)}) collective-permute-start(f32[3,1024,128]{2,1,0:T(8,128)} %get-tuple-element.24.late_ref), channel_id=1, source_target_pairs={{0,1},{1,2},{2,3},{3,4},{4,5},{5,6},{6,7},{7,0},{8,9},{9,10},{10,1... | collective-permute-start | bytes 4718600 | tf_op jit(solution)/shard_map/ppermute | solution.py:406
  60.0 7.3 %copy-start.2 = (bf16[12,256,256]{2,1,0:T(8,128)(2,1)}, bf16[12,256,256]{2,1,0:T(8,128)(2,1)S(1)}, u32[]{:S(2)}) copy-start(bf16[12,256,256]{2,1,0:T(8,128)(2,1)S(1)} %get-tuple-element.22.sides_ref) | copy-start | bytes 4718596
  61.6 5.6 %copy-start = (f32[3,1024,128]{2,1,0:T(8,128)}, f32[3,1024,128]{2,1,0:T(8,128)S(1)}, u32[]{:S(2)}) copy-start(f32[3,1024,128]{2,1,0:T(8,128)S(1)} %collective-permute-done.6.late_ref) | copy-start | bytes 4718596
  67.3 44.7 %collective-permute-start.11 = (f32[4,1024,128]{2,1,0:T(8,128)}, f32[4,1024,128]{2,1,0:T(8,128)}, u32[]{:S(2)}, u32[]{:S(2)}) collective-permute-start(f32[4,1024,128]{2,1,0:T(8,128)} %get-tuple-element.28.own_moved_ref), channel_id=1, source_target_pairs={{0,1},{1,2},{2,3},{3,4},{4,5},{5,6},{6,7},{7,0},{8,9},{9,10},{10,1... | collective-permute-start | bytes 6291464 | tf_op jit(solution)/shard_map/ppermute | solution.py:406
  76.3 4.4 %collective-permute-start.7 = (f32[136,128]{1,0:T(8,128)S(1)}, f32[136,128]{1,0:T(8,128)S(1)}, u32[]{:S(2)}, u32[]{:S(2)}) collective-permute-start(f32[136,128]{1,0:T(8,128)S(1)} %reduce_sum.19), channel_id=1, source_target_pairs={{0,32},{8,40},{16,48},{24,56},{32,0},{40,8},{48,16},{56,24},{64,96... | collective-permute-start | bytes 208904 | tf_op jit(solution)/shard_map/ppermute | solution.py:420
  80.7 6.3 %collective-permute-start.8 = (f32[136,128]{1,0:T(8,128)S(1)}, f32[136,128]{1,0:T(8,128)S(1)}, u32[]{:S(2)}, u32[]{:S(2)}) collective-permute-start(f32[136,128]{1,0:T(8,128)S(1)} %add.21), channel_id=1, source_target_pairs={{0,64},{8,72},{16,80},{24,88},{32,96},{40,104},{48,112},{56,120},{... | collective-permute-start | bytes 208904 | tf_op jit(solution)/shard_map/ppermute | solution.py:420
  87.0 7.4 %collective-permute-start.9 = (f32[136,128]{1,0:T(8,128)S(1)}, f32[136,128]{1,0:T(8,128)S(1)}, u32[]{:S(2)}, u32[]{:S(2)}) collective-permute-start(f32[136,128]{1,0:T(8,128)S(1)} %add.22), channel_id=1, source_target_pairs={{0,224},{8,232},{16,240},{24,248},{32,192},{40,200},{48,208},{56,2... | collective-permute-start | bytes 208904 | tf_op jit(solution)/shard_map/ppermute | solution.py:420
  94.4 5.0 %collective-permute-start.10 = (f32[136,128]{1,0:T(8,128)S(1)}, f32[136,128]{1,0:T(8,128)S(1)}, u32[]{:S(2)}, u32[]{:S(2)}) collective-permute-start(f32[136,128]{1,0:T(8,128)S(1)} %add.23), channel_id=1, source_target_pairs={{0,1},{1,2},{2,3},{3,4},{4,5},{5,6},{6,7},{7,0},{8,9},{9,10},{10,1... | collective-permute-start | bytes 208904 | tf_op jit(solution)/shard_map/ppermute | solution.py:406
  100.2 11.7 %all-to-all-start.3 = ((f32[4,2,136,128]{3,2,1,0:T(8,128)}), f32[4,2,136,128]{3,2,1,0:T(8,128)S(1)}, u32[]{:S(2)}, u32[]{:S(2)}) async-start(f32[4,2,136,128]{3,2,1,0:T(8,128)} %broadcast_in_dim.7), calls=%async_computation.3 | async-start | bytes 1114112 | tf_op jit(solution)/shard_map/all_to_all | solution.py:427
  105.1 1.4 %copy-start.1 = (f32[3,1024,128]{2,1,0:T(8,128)S(1)}, f32[3,1024,128]{2,1,0:T(8,128)}, u32[]{:S(2)}) copy-start(f32[3,1024,128]{2,1,0:T(8,128)} %copy-done) | copy-start | bytes 4718596
  106.5 1.4 %copy-start.3 = (bf16[12,256,256]{2,1,0:T(8,128)(2,1)S(1)}, bf16[12,256,256]{2,1,0:T(8,128)(2,1)}, u32[]{:S(2)}) copy-start(bf16[12,256,256]{2,1,0:T(8,128)(2,1)} %copy-done.2) | copy-start | bytes 4718596
